TPU v7x, 256 devices: a whole 4x4x8 slice. The times are simulated.
256 devices in a mesh: seq: 32 (over y, x, core), dp: 8 (over z).
Axes of the slice: x: 4, y: 4, z: 8, core: 2. Of those that a mesh axis runs over, the one named last changes fastest.
Arguments:
- mixer_input: bfloat16 [8, 8192, 2560], P('dp', 'seq'), may hold values from -6 to 6
- scan_input: bfloat16 [8, 8192, 2560], P('dp', 'seq'), may hold values from -6 to 6
- step_logits: float32 [8, 40, 8192], P('dp', None, 'seq'), may hold values from -2 to 5
- output_grad: bfloat16 [8, 8192, 2560], P('dp', 'seq'), may hold values from -6 to 6
- state_proj: bfloat16 [2560, 256], replicated, may hold values from -0.125 to 0.125
- step_bias: float32 [40], replicated, may hold values from -6 to -4
- rate_log: float32 [40], replicated, may hold values from -10 to 2
- direct_coefficient: float32 [40], replicated, may hold values from 0.5 to 1.5
Outputs:
- scan_grad: bfloat16 [8, 8192, 2560], P('dp', 'seq')
- logit_grad: float32 [8, 40, 8192], P('dp', None, 'seq')
- mixer_grad: bfloat16 [8, 8192, 2560], P('dp', 'seq')
- proj_grad: float32 [2560, 256], P('seq')
- rate_grad: float32 [40], replicated
- skip_grad: float32 [40], replicated
- bias_grad: float32 [40], replicated
All inputs are finite; a program needn't handle non-finite values.
Results may differ from a plain program's by a relative error of at most 0.0065.
Values sent between devices are 32-bit elements; how exact they have to be, the bound alone decides.
No kernel may reach another device: no remote copies, remote signals or barrier semaphores. Data moves between devices by JAX's collectives and lax.ppermute only.
A program may use at most 256 MiB of HBM per device.

v0:
```python
from functools import partial
import math

import jax
import jax.numpy as jnp
from jax import lax
from jax.sharding import PartitionSpec as P

exact_precision = lax.Precision.HIGHEST


def carried_in(part, axis, combine, identity, reverse):
    count = lax.axis_size(axis)
    place = lax.axis_index(axis)
    ahead = count - 1 - place if reverse else place
    gathered = jax.tree.map(lambda a: lax.all_gather(a, axis), part)
    state = jax.tree.map(lambda a, e: jnp.zeros_like(a) + jnp.asarray(e, a.dtype), part, identity)

    def one(turn, state):
        source = count - 1 - turn if reverse else turn
        return combine(
            state, jax.tree.map(lambda a: lax.dynamic_index_in_dim(a, source, 0, False), gathered)
        )

    return lax.fori_loop(0, ahead, one, state)


def decay_table(log_decay):
    length = log_decay.shape[1]
    causal_mask = jnp.arange(length)[:, None] >= jnp.arange(length)[None, :]
    log_gap = log_decay[:, :, None] - log_decay[:, None, :]
    return jnp.where(causal_mask[None], jnp.exp(jnp.where(causal_mask[None], log_gap, 0.0)), 0.0)


def discretization_intervals(logits, bias, rates_log):
    step_dt = jax.nn.softplus(logits + bias[:, None])
    log_decay = jnp.cumsum(-jnp.exp(rates_log)[:, None] * step_dt, axis=1)
    return (step_dt, log_decay)


def weighted_outer(weights, values, right_side):
    length, head_count, head_dim = values.shape
    scaled = (values * weights.T[:, :, None]).reshape(length, head_count * head_dim)
    product = lax.dot_general(
        scaled, right_side, (((0,), (0,)), ((), ())), precision=exact_precision
    )
    return product.reshape(head_count, head_dim, -1)


def group_forward(
    start_state, scores, inputs_part, logits, bias, rates_log, b_state, readout_memory
):
    head_count = logits.shape[0]
    length = inputs_part.shape[0]
    step_dt, log_decay = discretization_intervals(logits, bias, rates_log)
    x_scaled = inputs_part.reshape(length, head_count, -1) * step_dt.T[:, :, None]
    within = jnp.einsum(
        "hts,shp->thp", decay_table(log_decay) * scores[None], x_scaled, precision=exact_precision
    )
    carried = jnp.exp(log_decay).T[:, :, None] * jnp.einsum(
        "tn,hpn->thp", readout_memory, start_state, precision=exact_precision
    )
    final_log = log_decay[:, -1]
    end_state = jnp.exp(final_log)[:, None, None] * start_state + weighted_outer(
        jnp.exp(final_log[:, None] - log_decay), x_scaled, b_state
    )
    return ((within + carried).reshape(length, -1), end_state)


def group_summary(inputs_part, grads_part, logits, bias, rates_log, b_state, readout_memory):
    head_count = logits.shape[0]
    length = inputs_part.shape[0]
    step_dt, log_decay = discretization_intervals(logits, bias, rates_log)
    x_scaled = inputs_part.reshape(length, head_count, -1) * step_dt.T[:, :, None]
    final_log = log_decay[:, -1]
    local_end = weighted_outer(jnp.exp(final_log[:, None] - log_decay), x_scaled, b_state)
    start_grad = weighted_outer(
        jnp.exp(log_decay), grads_part.reshape(length, head_count, -1), readout_memory
    )
    return (jnp.exp(final_log), local_end, start_grad)


def combine_carry(earlier, trailing_portion):
    return (
        earlier[0] * trailing_portion[0],
        trailing_portion[0][:, None, None] * earlier[1] + trailing_portion[1],
    )


def contract_rows(left, right):
    return lax.dot_general(
        left, right, (((0,), (0,)), ((), ())), preferred_element_type=jnp.float32
    )


def on_device(
    mixer_input,
    scan_input,
    step_logits,
    output_grad,
    state_proj,
    step_bias,
    rate_log,
    direct_coefficient,
):
    tokens = mixer_input[0]
    x_local = scan_input[0]
    logits = step_logits[0]
    grads_in = output_grad[0]
    step_count, feature_width = x_local.shape
    head_count = step_bias.shape[0]
    head_dim = feature_width // head_count
    state_dim = state_proj.shape[1] // 2
    group_size = math.gcd(head_count, 8)
    group_count = head_count // group_size
    span = group_size * head_dim
    bc_round = jnp.dot(tokens, state_proj, preferred_element_type=jnp.float32).astype(jnp.bfloat16)
    b_state = bc_round[:, :state_dim].astype(jnp.float32)
    readout_memory = bc_round[:, state_dim:].astype(jnp.float32)
    scores = jnp.dot(readout_memory, b_state.T, precision=exact_precision)
    decay_parts = []
    state_parts = []
    back_parts = []
    for member in range(group_count):
        col_first = member * span
        head_first = member * group_size
        decay_part, state_part, back_part = group_summary(
            x_local[:, col_first : col_first + span].astype(jnp.float32),
            grads_in[:, col_first : col_first + span].astype(jnp.float32),
            logits[head_first : head_first + group_size],
            step_bias[head_first : head_first + group_size],
            rate_log[head_first : head_first + group_size],
            b_state,
            readout_memory,
        )
        decay_parts.append(decay_part)
        state_parts.append(state_part)
        back_parts.append(back_part)
    decay_all = jnp.concatenate(decay_parts, axis=0)
    state_all = jnp.concatenate(state_parts, axis=0)
    backward_total = jnp.concatenate(back_parts, axis=0)
    skip_local = jnp.sum(
        (x_local.astype(jnp.float32) * grads_in.astype(jnp.float32)).reshape(
            step_count, head_count, head_dim
        ),
        axis=(0, 2),
    )
    grad_scale = float(step_count * lax.axis_size("seq") * lax.axis_size("dp")) ** (-0.5)
    identity = (
        jnp.ones((head_count,), jnp.float32),
        jnp.zeros((head_count, head_dim, state_dim), jnp.float32),
    )
    start_states = carried_in((decay_all, state_all), "seq", combine_carry, identity, False)[1]
    end_grads = carried_in((decay_all, backward_total), "seq", combine_carry, identity, True)[1]
    score_gradient = jnp.zeros((step_count, step_count), jnp.float32)
    b_grad = jnp.zeros((step_count, state_dim), jnp.float32)
    c_grad = jnp.zeros((step_count, state_dim), jnp.float32)
    input_parts = []
    logit_parts = []
    bias_parts = []
    rate_parts = []
    for member in range(group_count):
        col_first = member * span
        head_first = member * group_size
        forward_fn = partial(group_forward, start_states[head_first : head_first + group_size])
        _, pullback = jax.vjp(
            forward_fn,
            scores,
            x_local[:, col_first : col_first + span].astype(jnp.float32),
            logits[head_first : head_first + group_size],
            step_bias[head_first : head_first + group_size],
            rate_log[head_first : head_first + group_size],
            b_state,
            readout_memory,
        )
        cotangents = pullback(
            (
                grads_in[:, col_first : col_first + span].astype(jnp.float32),
                end_grads[head_first : head_first + group_size],
            )
        )
        score_gradient = score_gradient + cotangents[0]
        input_parts.append(cotangents[1])
        logit_parts.append(cotangents[2])
        bias_parts.append(cotangents[3])
        rate_parts.append(cotangents[4])
        b_grad = b_grad + cotangents[5]
        c_grad = c_grad + cotangents[6]
    b_grad = b_grad + lax.dot_general(
        score_gradient, readout_memory, (((0,), (0,)), ((), ())), precision=exact_precision
    )
    c_grad = c_grad + jnp.dot(score_gradient, b_state, precision=exact_precision)
    grad_bc = jnp.concatenate([b_grad, c_grad], axis=1).astype(jnp.bfloat16)
    scan_grad = (
        jnp.concatenate(input_parts, axis=1)
        + jnp.repeat(direct_coefficient, head_dim)[None, :] * grads_in.astype(jnp.float32)
    ).astype(jnp.bfloat16)
    logit_grad = jnp.concatenate(logit_parts, axis=0)
    mixer_grad = lax.dot_general(
        grad_bc, state_proj, (((1,), (1,)), ((), ())), preferred_element_type=jnp.float32
    ).astype(jnp.bfloat16)
    local_weight = contract_rows(tokens, grad_bc)
    replica_weight = lax.psum(local_weight, "dp")
    proj_grad = (
        lax.psum_scatter(replica_weight, "seq", scatter_dimension=0, tiled=True) * grad_scale
    )
    rate_local = jnp.concatenate(rate_parts, axis=0)
    bias_local = jnp.concatenate(bias_parts, axis=0)
    rate_total, bias_total, skip_total = lax.psum(
        (rate_local, bias_local, skip_local), ("seq", "dp")
    )
    return (
        scan_grad[None],
        logit_grad[None],
        mixer_grad[None],
        proj_grad,
        rate_total * grad_scale,
        skip_total * grad_scale,
        bias_total * grad_scale,
    )


def solution(mesh):
    placed = (
        P("dp", "seq", None),
        P("dp", "seq", None),
        P("dp", None, "seq"),
        P("dp", "seq", None),
        P(),
        P(),
        P(),
        P(),
    )
    return jax.shard_map(
        on_device,
        mesh=mesh,
        in_specs=placed,
        out_specs=(
            P("dp", "seq", None),
            P("dp", None, "seq"),
            P("dp", "seq", None),
            P("seq", None),
            P(),
            P(),
            P(),
        ),
        check_vma=False,
    )
```

profile of v0, /device:TPU:2, one launch (start us, length us, event | category | flops | bytes accessed | tf_op | source)
XLA Modules:
  0.0 699.4 jit_solution(1624021152675142948)
XLA Ops:
  15.1 2.3 fusion.92
  31.3 65.0 %all-reduce.5 = f32[1280]{0:T(1024)S(1)} all-reduce(f32[1280]{0:T(1024)S(1)} %dynamic-update-slice), channel_id=2, replica_groups=mesh['seq'=32,'dp'=8] {'seq'}, use_global_device_ids=true, to_apply=%add.5 | all-reduce | flops 1280 | bytes 10240
  110.6 1.7 slice_convert_fusion.5
  116.8 7.4 %fusion.71 = (f32[8,256]{1,0:T(8,128)}, f32[8,256]{1,0:T(8,128)}, f32[256,256]{0,1:T(8,128)S(1)}, f32[256,256]{0,1:T(8,128)S(1)}, f32[8,256]{1,0:T(8,128)}, /*in...) fusion(f32[8,256]{1,0:T(8,128)S(1)} %get-tuple-element.280, ...), kind=kOutput, calls=%fused_computation.84 | convolution fusion | flops 431271936 | bytes 10944512 | tf_op jit(solution)/shard_map/transpose(jvp(hts,shp->thp))/dot_general | solution.py:57
  124.3 40.3 %all-gather.6.cloned.1.call-done = f32[1280,64,128]{2,1,0:T(8,128)} async-done(((f32[40,64,128]{2,1,0:T(8,128)}), f32[1280,64,128]{2,1,0:T(8,128)}) %all-gather.6.cloned.1.call-update) | async-done | bytes 41943056 | tf_op jit(solution)/shard_map/all_gather | solution.py:16
  164.7 67.9 %while.26 = (s32[]{:T(128)}, f32[40,64,128]{2,1,0:T(8,128)S(1)}, s32[]{:T(128)}, f32[32,40]{1,0:T(8,128)}, f32[32,40,64,128]{3,2,1,0:T(8,128)}, /*index=5*/s32[]{:T(128)}, s32[]{:T(128)}, s32[]{:T(128)}, s32[]{:T(128)}) while((s32[]{:T(128)}, f32[40,64,128]{2,1,0:T(8,128)S(1)}, s32[]{:T(128)}, f32[32,40]{1,0:T(8,128)}, ...), condition=%wide.region_11.12_spmd, body=%wide.region_10.11_spmd.sunk | while | flops 655366 | bytes 3932787 | solution.py:25
  179.2 1.8 bitcast_add_fusion.14
  216.4 2.0 bitcast_add_fusion.14
  219.1 2.0 bitcast_add_fusion.14
  237.4 69.7 %all-gather.8.cloned.1.call-done = f32[1280,64,128]{2,1,0:T(8,128)} async-done(((f32[40,64,128]{2,1,0:T(8,128)}), f32[1280,64,128]{2,1,0:T(8,128)}) %all-gather.8.cloned.1.call-update) | async-done | bytes 41943056 | tf_op jit(solution)/shard_map/all_gather | solution.py:16
  308.4 7.8 %while.27 = (s32[]{:T(128)}, f32[40,64,128]{2,1,0:T(8,128)}, s32[]{:T(128)}, f32[32,40]{1,0:T(8,128)}, f32[32,40,64,128]{3,2,1,0:T(8,128)}, /*index=5*/s32[]{:T(128)}, s32[]{:T(128)}, s32[]{:T(128)}) while((s32[]{:T(128)}, f32[40,64,128]{2,1,0:T(8,128)}, s32[]{:T(128)}, f32[32,40]{1,0:T(8,128)}, f32[32,40,64,128]{3,2,1,0:T(8,128)}, ...), condition=%wide.region_26.28_spmd, body=%wide.region_25.27_spmd.sunk | while | flops 655365 | bytes 3932767 | solution.py:25
  309.0 3.0 bitcast_add_fusion.15
  312.7 3.0 bitcast_add_fusion.15
  316.2 2.1 multiply_reduce_fusion.10
  319.6 2.3 convolution_bitcast_fusion.8
  321.9 3.1 fusion.78
  326.4 1.7 fusion.81
  329.9 3.7 multiply_reduce_fusion
  339.4 3.9 reduce-window.140
  354.9 3.7 reduce-window.136
  368.1 2.3 convolution_bitcast_fusion.7
  370.5 3.1 fusion.75
  375.7 4.5 multiply_reduce_fusion.1
  387.1 3.9 reduce-window.144
  399.1 1.8 convolution_bitcast_fusion.1
  400.9 1.7 convolution_bitcast_fusion.3
  409.4 2.0 convolution_bitcast_fusion
  411.4 3.2 copy.184
  418.6 2.5 reduce-window.134
  421.8 3.2 reduce-window.146
  435.6 179.8 %all-reduce.6 = (f32[40]{0:T(128)S(1)}, f32[40]{0:T(128)S(1)}, f32[40]{0:T(128)S(1)}) all-reduce(f32[40]{0:T(128)S(1)} %concatenate.47, f32[40]{0:T(128)S(1)} %reduce_sum.567, f32[40]{0:T(128)S(1)} %concatenate.48), channel_id=1, replica_groups=mesh['seq'=32,'dp'=8] {'seq','dp'}, use_global_device_ids=true, to_apply=%region_81.83 | all-reduce | flops 120 | bytes 960 | tf_op jit(solution)/shard_map/psum | solution.py:209
  620.3 70.7 %all-reduce.9.cloned.1.call-done = f32[80,256]{0,1:T(8,128)} async-done(((f32[80,256]{0,1:T(8,128)}), f32[80,256]{0,1:T(8,128)}) %all-reduce.9.cloned.1.call-update) | async-done | bytes 81936 | tf_op jit(solution)/shard_map/psum | solution.py:203
  (522 shorter events, 183.9 us)
Async XLA Ops:
  7.2 157.4 %all-gather.6.cloned.1.call-start = ((), (), s32[]{:S(2)}) async-start(), calls=%async_computation.1 | async-start | bytes 43253760 | tf_op jit(solution)/shard_map/all_gather | solution.py:16
  8.2 15.4 %copy-start.96 = (f32[8]{0:T(128)}, f32[8]{0:T(128)S(1)}, u32[]{:S(2)}) copy-start(f32[8]{0:T(128)S(1)} %get-tuple-element.370) | copy-start | bytes 100
  8.2 15.4 %copy-start.112 = (f32[8]{0:T(128)}, f32[8]{0:T(128)S(1)}, u32[]{:S(2)}) copy-start(f32[8]{0:T(128)S(1)} %get-tuple-element.363) | copy-start | bytes 100
  8.2 15.5 %copy-start.90 = (f32[8]{0:T(128)}, f32[8]{0:T(128)S(1)}, u32[]{:S(2)}) copy-start(f32[8]{0:T(128)S(1)} %get-tuple-element.372) | copy-start | bytes 100
  8.2 15.5 %copy-start.92 = (f32[8]{0:T(128)}, f32[8]{0:T(128)S(1)}, u32[]{:S(2)}) copy-start(f32[8]{0:T(128)S(1)} %get-tuple-element.373) | copy-start | bytes 100
  8.2 15.5 %copy-start.94 = (f32[8]{0:T(128)}, f32[8]{0:T(128)S(1)}, u32[]{:S(2)}) copy-start(f32[8]{0:T(128)S(1)} %get-tuple-element.374) | copy-start | bytes 100
  8.2 15.5 %copy-start.102 = (f32[8]{0:T(128)}, f32[8]{0:T(128)S(1)}, u32[]{:S(2)}) copy-start(f32[8]{0:T(128)S(1)} %get-tuple-element.360) | copy-start | bytes 100
  8.3 15.5 %copy-start.104 = (f32[8]{0:T(128)}, f32[8]{0:T(128)S(1)}, u32[]{:S(2)}) copy-start(f32[8]{0:T(128)S(1)} %get-tuple-element.361) | copy-start | bytes 100
  8.3 15.5 %copy-start.106 = (f32[8]{0:T(128)}, f32[8]{0:T(128)S(1)}, u32[]{:S(2)}) copy-start(f32[8]{0:T(128)S(1)} %get-tuple-element.359) | copy-start | bytes 100
  8.3 15.5 %copy-start.108 = (f32[8]{0:T(128)}, f32[8]{0:T(128)S(1)}, u32[]{:S(2)}) copy-start(f32[8]{0:T(128)S(1)} %get-tuple-element.362) | copy-start | bytes 100
  8.3 15.5 %copy-start.110 = (f32[8]{0:T(128)}, f32[8]{0:T(128)S(1)}, u32[]{:S(2)}) copy-start(f32[8]{0:T(128)S(1)} %get-tuple-element.371) | copy-start | bytes 100
  20.6 286.5 %all-gather.8.cloned.1.call-start = ((), (), s32[]{:S(2)}) async-start(), calls=%async_computation.2 | async-start | bytes 43253760 | tf_op jit(solution)/shard_map/all_gather | solution.py:16
  22.3 87.1 %copy-start.1 = (bf16[1,256,2560]{1,2,0:T(8,128)(2,1)}, bf16[1,256,2560]{1,2,0:T(8,128)(2,1)S(1)}, u32[]{:S(2)}) copy-start(bf16[1,256,2560]{1,2,0:T(8,128)(2,1)S(1)} %copy.166) | copy-start | bytes 3932164
  23.8 91.8 %copy-start.61 = (f32[256,8]{0,1:T(8,128)}, f32[256,8]{0,1:T(8,128)S(1)}, u32[]{:S(2)}) copy-start(f32[256,8]{0,1:T(8,128)S(1)} %get-tuple-element.326) | copy-start | bytes 24580
  23.9 88.5 %copy-start.49 = (f32[256,8]{0,1:T(8,128)}, f32[256,8]{0,1:T(8,128)S(1)}, u32[]{:S(2)}) copy-start(f32[256,8]{0,1:T(8,128)S(1)} %get-tuple-element.346) | copy-start | bytes 24580
  23.9 92.8 %copy-start.63 = (f32[256,8]{0,1:T(8,128)}, f32[256,8]{0,1:T(8,128)S(1)}, u32[]{:S(2)}) copy-start(f32[256,8]{0,1:T(8,128)S(1)} %get-tuple-element.324) | copy-start | bytes 24580
  26.4 74.5 %copy-start.127 = (f32[40]{0:T(128)S(1)}, f32[40]{0:T(128)}, u32[]{:S(2)}) copy-start(f32[40]{0:T(128)} %param.20) | copy-start | bytes 484
  29.7 589.0 %reduce-scatter.4.cloned.1.call-start = ((), (), s32[]{:S(2)}) async-start(), calls=%async_computation.4 | async-start | bytes 2703360
  102.3 14.4 %copy-start.59 = (f32[8,256]{1,0:T(8,128)}, f32[8,256]{1,0:T(8,128)S(1)}, u32[]{:S(2)}) copy-start(f32[8,256]{1,0:T(8,128)S(1)} %get-tuple-element.276) | copy-start | bytes 24580
  103.2 13.5 %copy-start.57 = (f32[8,256]{1,0:T(8,128)}, f32[8,256]{1,0:T(8,128)S(1)}, u32[]{:S(2)}) copy-start(f32[8,256]{1,0:T(8,128)S(1)} %get-tuple-element.274) | copy-start | bytes 24580
  104.0 12.7 %copy-start.51 = (f32[8,256]{1,0:T(8,128)}, f32[8,256]{1,0:T(8,128)S(1)}, u32[]{:S(2)}) copy-start(f32[8,256]{1,0:T(8,128)S(1)} %get-tuple-element.272) | copy-start | bytes 24580
  104.9 11.8 %copy-start.69 = (f32[8,256]{1,0:T(8,128)}, f32[8,256]{1,0:T(8,128)S(1)}, u32[]{:S(2)}) copy-start(f32[8,256]{1,0:T(8,128)S(1)} %get-tuple-element.280) | copy-start | bytes 24580
  333.6 36.8 %copy-start.55 = (f32[8,256]{1,0:T(8,128)S(1)}, f32[8,256]{1,0:T(8,128)}, u32[]{:S(2)}) copy-start(f32[8,256]{1,0:T(8,128)} %copy-done.54) | copy-start | bytes 24580
  375.7 20.6 %copy-start.53 = (f32[8,256]{1,0:T(8,128)S(1)}, f32[8,256]{1,0:T(8,128)}, u32[]{:S(2)}) copy-start(f32[8,256]{1,0:T(8,128)} %copy-done.51) | copy-start | bytes 24580
  414.6 12.3 %copy-start.19 = (f32[256,8,64]{0,2,1:T(8,128)S(1)}, f32[256,8,64]{0,2,1:T(8,128)}, u32[]{:S(2)}) copy-start(f32[256,8,64]{0,2,1:T(8,128)} %get-tuple-element.321) | copy-start | bytes 1572868
  414.7 13.3 %copy-start.18 = (f32[256,8,64]{0,2,1:T(8,128)S(1)}, f32[256,8,64]{0,2,1:T(8,128)}, u32[]{:S(2)}) copy-start(f32[256,8,64]{0,2,1:T(8,128)} %get-tuple-element.320) | copy-start | bytes 1572868
  414.7 14.3 %copy-start.17 = (f32[256,8,64]{0,2,1:T(8,128)S(1)}, f32[256,8,64]{0,2,1:T(8,128)}, u32[]{:S(2)}) copy-start(f32[256,8,64]{0,2,1:T(8,128)} %get-tuple-element.319) | copy-start | bytes 1572868
  414.7 276.4 %all-reduce.9.cloned.1.call-start = ((), (), s32[]{:S(2)}) async-start(), calls=%async_computation.3 | async-start | bytes 262144 | tf_op jit(solution)/shard_map/psum | solution.py:203
  432.5 182.9 %copy-start.25 = (bf16[2560,256]{1,0:T(8,128)(2,1)S(1)}, bf16[2560,256]{1,0:T(8,128)(2,1)}, u32[]{:S(2)}) copy-start(bf16[2560,256]{1,0:T(8,128)(2,1)} %param.17) | copy-start | bytes 3932164
  432.5 182.9 %copy-start.35 = (bf16[256,128]{0,1:T(8,128)(2,1)S(1)}, bf16[256,128]{0,1:T(8,128)(2,1)}, u32[]{:S(2)}) copy-start(bf16[256,128]{0,1:T(8,128)(2,1)} %copy-done.34) | copy-start | bytes 196612
  432.6 182.9 %copy-start.37 = (bf16[256,128]{0,1:T(8,128)(2,1)S(1)}, bf16[256,128]{0,1:T(8,128)(2,1)}, u32[]{:S(2)}) copy-start(bf16[256,128]{0,1:T(8,128)(2,1)} %copy-done.36) | copy-start | bytes 196612
  620.3 72.4 %copy-start.126 = (f32[40,256]{1,0:T(8,128)}, f32[40,256]{1,0:T(8,128)S(1)}, u32[]{:S(2)}) copy-start(f32[40,256]{1,0:T(8,128)S(1)} %constant_dynamic-update-slice_fusion.5) | copy-start | bytes 122884
  (101 other events, 354.7 us)
Sparse Core Ops, SparseCore 0:
  20.7 143.7 all-gather.5
  167.1 139.9 all-gather.7
  414.8 191.3 reduce-scatter.3
  620.4 70.5 all-reduce.8
where the time goes:
time: 708 us; the launch traced here: 699 us
  blocking collectives  245 us (35%)
  waiting for transfers between devices  181 us (26%)
  other arithmetic  113 us (16%)
  matrix products  71.4 us (10%)
  local copies, waits for them, and re-layouts  71.2 us (10%)
  between operations  16.6 us (2%)
    psum x1, blocking collectives, on_device(): lax.psum((rate_local, bias_local, skip_local), ('seq', 'dp'))  180 us
    all_gather x2, waiting for transfers between devices, carried_in(): gathered = jax.tree.map(lambda a: lax.all_gather(a, axis), part)  110 us
    psum x1, waiting for transfers between devices, on_device(): replica_weight = lax.psum(local_weight, 'dp')  70.7 us
    unnamed x1, blocking collectives  65 us
    add x31, other arithmetic, combine_carry(): trailing_portion[0][:, None, None] * earlier[1] + trailing_portion[1]  52.6 us
    another operation x35, other arithmetic  33 us
    dot_general x10, matrix products, group_forward(): jnp.einsum('hts,shp->thp', decay_table(log_decay) * scores[None], x_scale...  25.7 us
    dot_general x20, matrix products, weighted_outer(): lax.dot_general(scaled, right_side, (((0,), (0,)), ((), ())), precision=e...  23.5 us
  transfers between devices with their start and end apart: 4, of which 3 were waited for; matrix products, arithmetic and copies ran while one was open for 19% of the time, Pallas kernels for 0%

commit v1 on v0

v1 whole, which is shorter than its diff:
```python
from functools import partial

import jax
import jax.numpy as jnp
from jax import lax
from jax.sharding import PartitionSpec as P
import jax.experimental.pallas as pl
import jax.experimental.pallas.tpu as pltpu

f32 = jnp.float32
bf16 = jnp.bfloat16

T = 256
H = 40
HD = 64
W = 2560
N = 128
HALF = 64
TAIL = 128
CHIPS = 16
ROWS = 80
PROWS = 88


def iota(shape, dim):
    return lax.broadcasted_iota(jnp.int32, shape, dim)


def split3(v):
    hi = v.astype(bf16).astype(f32)
    rest = v - hi
    mid = rest.astype(bf16).astype(f32)
    return hi, mid, rest - mid


def dot00(a, b):
    return lax.dot_general(a, b, (((0,), (0,)), ((), ())), preferred_element_type=f32)


def dot11(a, b):
    return lax.dot_general(a, b, (((1,), (1,)), ((), ())), preferred_element_type=f32)


def dot10(a, b):
    return lax.dot_general(a, b, (((1,), (0,)), ((), ())), preferred_element_type=f32)


def head_rows(count):
    lane_head = iota((count, W), 1) >> 6
    row = iota((count, W), 0)
    hit = (lane_head == row) | (lane_head == row - H) | (lane_head == row - 2 * H)
    return jnp.where(hit, 1.0, 0.0).astype(bf16)


def widen(v, spread):
    parts = jnp.concatenate(split3(v) + (jnp.zeros((8, T), f32),), axis=0).astype(bf16)
    return dot00(parts, spread)


def widen_row(row, spread):
    parts = jnp.concatenate(split3(row) + (jnp.zeros((8, 128), f32),), axis=0).astype(bf16)
    lanes = iota((N, W), 0) < H
    once = jnp.where(lanes, spread.astype(f32), 0.0).astype(bf16)
    out = dot10(parts, once)
    return out[0:8] + out[8:16] + out[16:24]


def column(row, count):
    eye = iota((count, count), 0) == iota((count, count), 1)
    return jnp.sum(jnp.where(eye, row, 0.0), axis=1, keepdims=True)


def over_positions(v, keep):
    parts = jnp.concatenate(split3(v) + (jnp.zeros((8, T), f32),), axis=0).astype(bf16)
    out = dot10(parts, jnp.where(keep, 1.0, 0.0).astype(bf16))
    return out[0:H] + out[H : 2 * H] + out[2 * H : 3 * H]


def step_sizes(logits, bias_row):
    z = logits + column(bias_row, H)
    e = jnp.exp(-jnp.abs(z))
    r = e / (2.0 + e)
    r2 = r * r
    poly = 1.0 / 17.0
    for odd in (15, 13, 11, 9, 7, 5, 3):
        poly = poly * r2 + 1.0 / odd
    dt = jnp.maximum(z, 0.0) + 2.0 * (r + r * r2 * poly)
    sig = jnp.where(z >= 0.0, 1.0, e) / (1.0 + e)
    return dt, sig


def summary_kernel(
    core_ref, tok_ref, x_ref, g_ref, proj_ref, logit_ref, bias_ref, rate_ref,
    bc_ref, xw_ref, ge_ref, keep_ref, send_ref, log_ref, dt_ref, sig_ref,
    both,
):
    bc = dot10(tok_ref[...], proj_ref[...]).astype(bf16)
    bc_ref[...] = bc
    dt, sig = step_sizes(logit_ref[...], bias_ref[...])
    rate = jnp.exp(column(rate_ref[...], H))
    log_decay = over_positions(-rate * dt, iota((T, T), 0) <= iota((T, T), 1))
    last = log_decay[:, T - 1 : T]
    log_ref[...] = log_decay
    dt_ref[...] = dt
    sig_ref[...] = sig
    spread = head_rows(N)
    xw = (x_ref[...].astype(f32) * widen(jnp.exp(last - log_decay) * dt, spread)).astype(bf16)
    xw_ref[...] = xw
    ge = (g_ref[...].astype(f32) * widen(jnp.exp(log_decay), spread)).astype(bf16)
    ge_ref[...] = ge
    both[0:N, :] = dot00(bc[:, :N], xw)
    both[N : 2 * N, :] = dot00(bc[:, N:], ge)
    mine = pl.multiple_of(core_ref[0] * HALF, HALF)
    theirs = pl.multiple_of(HALF - core_ref[0] * HALF, HALF)
    keep_ref[0:HALF, 0:W] = both[pl.ds(mine, HALF), :]
    keep_ref[HALF:N, 0:W] = both[pl.ds(N + mine, HALF), :]
    send_ref[0:HALF, 0:W] = both[pl.ds(theirs, HALF), :]
    send_ref[HALF:N, 0:W] = both[pl.ds(N + theirs, HALF), :]
    on_lane = iota((H, TAIL), 0) == iota((H, TAIL), 1)
    decay = jnp.exp(jnp.sum(jnp.where(on_lane, last, 0.0), axis=0, keepdims=True))
    decay = jnp.broadcast_to(decay, (N, TAIL))
    keep_ref[:, W:] = decay
    send_ref[:, W:] = decay


def chip_kernel(core_ref, keep_ref, got_ref, out_ref):
    spread = head_rows(N)
    decay_mine = keep_ref[0:8, W:]
    decay_their = got_ref[0:8, W:]
    wide_mine = widen_row(decay_mine, spread)[0:1]
    wide_their = widen_row(decay_their, spread)[0:1]
    first = core_ref[0] == 0
    one = jnp.ones((1, W), f32)
    a = jnp.where(first, wide_their, one)
    b = jnp.where(first, one, wide_mine)
    c = jnp.where(first, one, wide_their)
    d = jnp.where(first, wide_mine, one)
    out_ref[0:HALF, 0:W] = a * keep_ref[0:HALF, 0:W] + b * got_ref[0:HALF, 0:W]
    out_ref[HALF:N, 0:W] = c * keep_ref[HALF:N, 0:W] + d * got_ref[HALF:N, 0:W]
    out_ref[:, W:] = keep_ref[:, W:] * got_ref[:, W:]


def scan_kernel(back_ref, in_ref, after_ref, out_ref, wide):
    spread = head_rows(N)
    for c in range(CHIPS):
        wide[c] = widen_row(in_ref[c, :, W:], spread)
    back = back_ref[0]
    state = jnp.zeros((8, W), f32)
    for i in range(CHIPS):
        c = jnp.where(back == 1, CHIPS - 1 - i, i)
        out_ref[c] = state
        state = wide[c] * state + in_ref[c, :, 0:W]


def core_kernel(core_ref, chip_ref, keep_ref, got_ref, mine_ref, send_ref):
    spread = head_rows(N)
    wide_mine = widen_row(keep_ref[0:8, W:], spread)[0:1]
    wide_their = widen_row(got_ref[0:8, W:], spread)[0:1]
    s = chip_ref[0:HALF, :]
    e = chip_ref[HALF:N, :]

    @pl.when(core_ref[0] == 0)
    def _():
        mine_ref[0:HALF, :] = s
        mine_ref[HALF:N, :] = wide_their * e + got_ref[HALF:N, 0:W]
        send_ref[0:HALF, :] = wide_mine * s + keep_ref[0:HALF, 0:W]
        send_ref[HALF:N, :] = e

    @pl.when(core_ref[0] == 1)
    def _():
        mine_ref[0:HALF, :] = wide_their * s + got_ref[0:HALF, 0:W]
        mine_ref[HALF:N, :] = e
        send_ref[0:HALF, :] = s
        send_ref[HALF:N, :] = wide_mine * e + keep_ref[HALF:N, 0:W]


def within_kernel(
    tok_ref, x_ref, g_ref, bc_ref, log_ref, dt_ref,
    du_ref, sg_ref, cross_ref, col_ref, skip_ref, tokt_ref,
    wide_log, late_log, ds, rows,
):
    half = T // 2
    spread = head_rows(N)
    log_decay = log_ref[...]
    dt = dt_ref[...]
    wide_log[...] = widen(log_decay, spread)
    late_log[...] = log_decay - jnp.log(dt)
    b = bc_ref[:, :N]
    c = bc_ref[:, N:]
    scores = dot11(c, b)
    ds[...] = jnp.zeros((T, T), f32)
    rows[...] = jnp.zeros((T, 128), f32)
    causal = iota((half, half), 0) >= iota((half, half), 1)
    lane = iota((T, 128), 1)

    def pair(i, carry):
        cols = pl.ds(pl.multiple_of(i * 128, 128), 128)
        xp = x_ref[:, cols]
        gp = g_ref[:, cols]
        logs = wide_log[:, cols]
        total = jnp.zeros((T, 128), f32)
        for m in range(2):
            h = 2 * i + m
            gm = jnp.where((lane >= HD) == (m == 1), gp.astype(f32), 0.0).astype(bf16)
            q0 = dot11(gm[0:half], xp[0:half])
            q1 = dot11(gm[half:], xp)
            late = late_log[pl.ds(h, 1), :]
            lc = logs[:, m * HD : m * HD + 1]
            gap0 = lc[0:half] - late[:, 0:half]
            gap1 = lc[half:] - late[:, half:]
            dec0 = jnp.exp(jnp.where(causal, gap0, -1e30))
            dec1 = jnp.concatenate(
                [
                    jnp.exp(lc[half:] - late[:, 0:half]),
                    jnp.exp(jnp.where(causal, gap1, -1e30)),
                ],
                axis=1,
            )
            m0 = dec0 * scores[0:half, 0:half]
            m1 = dec1 * scores[half:, :]
            ds[0:half, 0:half] += dec0 * q0
            ds[half:, :] += dec1 * q1
            p0 = m0 * q0
            p1 = m1 * q1
            rsum = jnp.concatenate(
                [jnp.sum(p0, axis=1, keepdims=True), jnp.sum(p1, axis=1, keepdims=True)], axis=0
            )
            rows[...] += jnp.where(lane == h, rsum, 0.0)
            csum1 = jnp.sum(p1, axis=0, keepdims=True)
            csum0 = jnp.sum(p0, axis=0, keepdims=True)
            col_ref[pl.ds(h, 1), :] = csum1 + jnp.concatenate(
                [csum0, jnp.zeros((1, half), f32)], axis=1
            )
            m1b = m1.astype(bf16)
            early = dot00(m0.astype(bf16), gm[0:half])
            both = dot00(m1b, gm[half:])
            total = total + both + jnp.concatenate([early, jnp.zeros((half, 128), f32)], axis=0)
        du_ref[:, cols] = total
        return carry

    lax.fori_loop(0, H // 2, pair, 0)
    hi, mid, _ = split3(ds[...])
    hi = hi.astype(bf16)
    mid = mid.astype(bf16)
    sg_ref[:, :N] = dot00(hi, c) + dot00(mid, c)
    sg_ref[:, N:] = dot10(hi, b) + dot10(mid, b)
    cross_ref[...] = rows[...].T[0:H, :] - col_ref[...]
    xg = x_ref[...].astype(f32) * g_ref[...].astype(f32)
    part = jnp.sum(xg.reshape(T // 8, 8, W), axis=0)
    skip = dot11(jnp.concatenate(split3(part), axis=0).astype(bf16), spread)
    skip = jnp.sum(skip, axis=0, keepdims=True)
    skip_ref[...] = jnp.broadcast_to(jnp.where(iota((1, 128), 1) < H, skip, 0.0), (8, 128))
    tokt_ref[...] = tok_ref[...].T


def gradient_kernel(
    core_ref, mine_ref, got_ref, xw_ref, ge_ref, x_ref, g_ref, bc_ref, proj_ref, tokt_ref,
    log_ref, dt_ref, sig_ref, rate_ref, direct_ref, du_ref, sgin_ref, cross_ref, col_ref, skip_ref,
    scan_ref, logit_ref, mixer_ref, keep_ref, send_ref,
    s_all, e_all, weight,
):
    spread = head_rows(N)
    core = core_ref[0]
    own = pl.multiple_of(core * HALF, HALF)
    other = pl.multiple_of(HALF - core * HALF, HALF)
    s_all[pl.ds(own, HALF), :] = mine_ref[0:HALF, :].astype(bf16)
    s_all[pl.ds(other, HALF), :] = got_ref[0:HALF, :].astype(bf16)
    e_all[pl.ds(own, HALF), :] = mine_ref[HALF:N, :].astype(bf16)
    e_all[pl.ds(other, HALF), :] = got_ref[HALF:N, :].astype(bf16)
    b = bc_ref[:, :N]
    c = bc_ref[:, N:]
    xw = xw_ref[...]
    ge = ge_ref[...]
    sg_b = sgin_ref[:, :N] + dot11(xw, e_all[...])
    sg_c = sgin_ref[:, N:] + dot11(ge, s_all[...])
    sg = jnp.concatenate([sg_b, sg_c], axis=1).astype(bf16)
    weight[...] = dot10(tokt_ref[...], sg)
    mixer_ref[...] = dot11(sg, proj_ref[...]).astype(bf16)
    log_decay = log_ref[...]
    dt = dt_ref[...]
    last = log_decay[:, T - 1 : T]
    to_end = widen(jnp.exp(last - log_decay) * dt, spread)
    eb = dot10(b, e_all[...])
    direct_row = jnp.broadcast_to(
        jnp.concatenate([direct_ref[...], jnp.zeros((1, 128 - H), f32)], axis=1), (8, 128)
    )
    direct = widen_row(direct_row, spread)[0:1]
    scan_ref[...] = (du_ref[...] + to_end * eb + direct * g_ref[...].astype(f32)).astype(bf16)
    pick = spread[0:48]
    v = dot11(pick, (xw.astype(f32) * eb).astype(bf16))[0:H]
    from_start = dot10(c, s_all[...])
    carry = dot11(pick, (ge.astype(f32) * from_start).astype(bf16))[0:H]
    meet = mine_ref[0:HALF, :] * mine_ref[HALF:N, :] + got_ref[0:HALF, :] * got_ref[HALF:N, :]
    meet = jnp.sum(meet.reshape(HALF // 8, 8, W), axis=0)
    meet = dot11(pick, jnp.concatenate(split3(meet), axis=0).astype(bf16))[0:H]
    through = jnp.sum(meet, axis=1, keepdims=True) * jnp.exp(last)
    row = iota((T, T), 0)
    col = iota((T, T), 1)
    log_grad = (
        through
        + over_positions(carry + cross_ref[...], row >= col)
        + over_positions(v, row < col)
    )
    rate = jnp.exp(column(rate_ref[...], H))
    dt_grad = (col_ref[...] + v) / dt - rate * log_grad
    logit = dt_grad * sig_ref[...]
    logit_ref[...] = logit
    on_lane = iota((H, 128), 0) == iota((H, 128), 1)

    def as_row(colsum):
        return jnp.sum(jnp.where(on_lane, colsum, 0.0), axis=0, keepdims=True)

    rate_row = as_row(jnp.sum(-rate * dt * log_grad, axis=1, keepdims=True))
    bias_row = as_row(jnp.sum(logit, axis=1, keepdims=True))
    params = jnp.concatenate(
        [
            jnp.concatenate([rate_row, bias_row], axis=1),
            jnp.concatenate([skip_ref[0:1, :], jnp.zeros((1, 128), f32)], axis=1),
            jnp.zeros((6, 256), f32),
        ],
        axis=0,
    )
    for chip in range(CHIPS):
        mine = pl.multiple_of((2 * chip + core) * ROWS, 8)
        theirs = pl.multiple_of((2 * chip + 1 - core) * ROWS, 8)
        keep_ref[chip, 0:ROWS, :] = weight[pl.ds(mine, ROWS), :]
        send_ref[chip, 0:ROWS, :] = weight[pl.ds(theirs, ROWS), :]
        keep_ref[chip, ROWS:PROWS, :] = params
        send_ref[chip, ROWS:PROWS, :] = params


def call(kernel, outs, scratch=(), smem=1, flops=0, moved=0, n_in=0):
    vmem = pl.BlockSpec(memory_space=pltpu.VMEM)
    return pl.pallas_call(
        kernel,
        out_shape=[jax.ShapeDtypeStruct(s, d) for s, d in outs],
        in_specs=[pl.BlockSpec(memory_space=pltpu.SMEM)] * smem + [vmem] * n_in,
        out_specs=[vmem] * len(outs),
        scratch_shapes=list(scratch),
        compiler_params=pltpu.CompilerParams(vmem_limit_bytes=48 * 1024 * 1024),
        cost_estimate=pl.CostEstimate(flops=flops, bytes_accessed=moved, transcendentals=0),
    )


def on_device(tokens, scan_input, logits, grads, proj, bias, rate_log, direct):
    tok, x, lg, g = tokens[0], scan_input[0], logits[0], grads[0]
    place = lax.axis_index("seq")
    core = lax.rem(place, 2).astype(jnp.int32).reshape(1)
    chip = lax.div(place, 2)
    back = (chip >= CHIPS // 2).astype(jnp.int32).reshape(1)
    bias_row = bias.reshape(1, H)
    rate_row = rate_log.reshape(1, H)
    direct_row = direct.reshape(1, H)
    swap = [(i, i ^ 1) for i in range(2 * CHIPS)]
    same_core = [[2 * i + k for i in range(CHIPS)] for k in range(2)]
    exchange = partial(
        lax.all_to_all, axis_name="seq", split_axis=0, concat_axis=0, axis_index_groups=same_core
    )

    bc, xw, ge, keep, send, log_decay, dt, sig = call(
        summary_kernel,
        [
            ((T, 2 * N), bf16), ((T, W), bf16), ((T, W), bf16),
            ((N, W + TAIL), f32), ((N, W + TAIL), f32),
            ((H, T), f32), ((H, T), f32), ((H, T), f32),
        ],
        [pltpu.VMEM((2 * N, W), f32)],
        n_in=7, flops=int(1e9), moved=int(1e7),
    )(core, tok, x, g, proj, lg, bias_row, rate_row)
    got = lax.ppermute(send, "seq", swap)
    (chips,) = call(
        chip_kernel, [((N, W + TAIL), f32)], n_in=2, flops=int(1e7), moved=int(4e6)
    )(core, keep, got)
    owned = exchange(chips.reshape(CHIPS, 8, W + TAIL))
    du, sg_in, cross, col, skip, tokt = call(
        within_kernel,
        [
            ((T, W), f32), ((T, 2 * N), f32), ((H, T), f32), ((H, T), f32), ((8, 128), f32),
            ((W, T), bf16),
        ],
        [
            pltpu.VMEM((T, W), f32), pltpu.VMEM((H, T), f32),
            pltpu.VMEM((T, T), f32), pltpu.VMEM((T, 128), f32),
        ],
        smem=0, n_in=6, flops=int(8e9), moved=int(1e7),
    )(tok, x, g, bc, log_decay, dt)
    (starts,) = call(
        scan_kernel, [((CHIPS, 8, W), f32)], [pltpu.VMEM((CHIPS, 8, W), f32)], n_in=2,
        flops=int(1e7), moved=int(3e6),
    )(back, owned, skip)
    returned = exchange(starts).reshape(N, W)
    mine, send2 = call(
        core_kernel, [((N, W), f32), ((N, W), f32)], n_in=3, flops=int(1e7), moved=int(6e6)
    )(core, returned, keep, got)
    got2 = lax.ppermute(send2, "seq", swap)
    scan_grad, logit_grad, mixer_grad, wkeep, wsend = call(
        gradient_kernel,
        [
            ((T, W), bf16), ((H, T), f32), ((T, W), bf16),
            ((CHIPS, PROWS, 2 * N), f32), ((CHIPS, PROWS, 2 * N), f32),
        ],
        [pltpu.VMEM((N, W), bf16), pltpu.VMEM((N, W), bf16), pltpu.VMEM((W, 2 * N), f32)],
        n_in=19, flops=int(3e9), moved=int(2e7),
    )(
        core, mine, got2, xw, ge, x, g, bc, proj, tokt, log_decay, dt, sig, rate_row, direct_row,
        du, sg_in, cross, col, skip,
    )
    wsum = wkeep + lax.ppermute(wsend, "seq", swap)
    total = jnp.sum(exchange(wsum), axis=0)
    for k in (1, 2, 4):
        total = total + lax.ppermute(total, "dp", [(i, i ^ k) for i in range(8)])
    total = total * (float(T * 2 * CHIPS * 8) ** -0.5)
    return (
        scan_grad[None],
        logit_grad[None],
        mixer_grad[None],
        total[0:ROWS],
        total[ROWS, 0:H],
        total[ROWS + 1, 0:H],
        total[ROWS, N : N + H],
    )


def solution(mesh):
    placed = (
        P("dp", "seq", None),
        P("dp", "seq", None),
        P("dp", None, "seq"),
        P("dp", "seq", None),
        P(),
        P(),
        P(),
        P(),
    )
    return jax.shard_map(
        on_device,
        mesh=mesh,
        in_specs=placed,
        out_specs=(
            P("dp", "seq", None),
            P("dp", None, "seq"),
            P("dp", "seq", None),
            P("seq", None),
            P(),
            P(),
            P(),
        ),
        check_vma=False,
    )
```

time: 708 us -> 142 us (0.20)
  blocking collectives: 245 us -> 48.9 us
  waiting for transfers between devices: 181 us -> 19.6 us
  other arithmetic: 113 us -> 1.68 us
  matrix products: 71.4 us -> 0 us
  local copies, waits for them, and re-layouts: 71.2 us -> 13.6 us
  Pallas kernels: 0 us -> 34.5 us
  starting transfers between devices: 0.16 us -> 21.3 us
  between operations: 16.6 us -> 0.75 us
    psum x1 -> x0, blocking collectives: 180 us -> none  [on_device(): lax.psum((rate_local, bias_local, skip_local), ('seq', 'dp'))]
    all_gather x2 -> x0, waiting for transfers between devices: 110 us -> none  [carried_in(): gathered = jax.tree.map(lambda a: lax.all_gather(a, axis), part)]
    dot_general x46 -> x0, matrix products: 71.4 us -> none  [the longest x10 25.7 us: group_forward(): jnp.einsum('hts,shp->thp', decay_table(log_decay) * scores[None], x_scale...]
    psum x1 -> x0, waiting for transfers between devices: 70.7 us -> none  [on_device(): replica_weight = lax.psum(local_weight, 'dp')]
    unnamed x1 -> x0, blocking collectives: 65 us -> none
    add x32 -> x3, other arithmetic: 52.7 us -> 1.58 us  [the longest x1 1.55 us: on_device(): wsum = wkeep + lax.ppermute(wsend, 'seq', swap)]
    all_to_all x0 -> x2, blocking collectives: none -> 48.9 us  [the longest x1 24.6 us: on_device(): total = jnp.sum(exchange(wsum), axis=0)]
    pallas_call x0 -> x6, Pallas kernels: none -> 34.5 us  [the longest x1 13.7 us: on_device(): call(within_kernel, [((T, W), f32), ((T, 2 * N), f32), ((H, T), f32), ((H...]
  transfers between devices with their start and end apart: 4 -> 7, of which waited for: 3 -> 7; matrix products, arithmetic and copies ran while one was open for 19% -> 0% of each run, Pallas kernels for 0% -> 10%
where the time goes in v1:
time: 142 us; the launch traced here: 140 us
  blocking collectives  48.9 us (34%)
  Pallas kernels  34.5 us (24%)
  starting transfers between devices  21.3 us (15%)
  waiting for transfers between devices  19.6 us (14%)
  local copies, waits for them, and re-layouts  13.6 us (10%)
  other arithmetic  1.68 us (1%)
    all_to_all x1, blocking collectives, on_device(): total = jnp.sum(exchange(wsum), axis=0)  24.6 us
    all_to_all x1, blocking collectives, on_device(): returned = exchange(starts).reshape(N, W)  24.4 us
    pallas_call x1, Pallas kernels, on_device(): call(within_kernel, [((T, W), f32), ((T, 2 * N), f32), ((H, T), f32), ((H...  13.7 us
    ppermute x3, starting transfers between devices, on_device(): total = total + lax.ppermute(total, 'dp', [(i, i ^ k) for i in range(8)])  13.3 us
    unnamed x36, local copies, waits for them, and re-layouts  12.4 us
    pallas_call x1, Pallas kernels, on_device(): call(gradient_kernel, [((T, W), bf16), ((H, T), f32), ((T, W), bf16), ((C...  10.7 us
    ppermute x3, waiting for transfers between devices, on_device(): total = total + lax.ppermute(total, 'dp', [(i, i ^ k) for i in range(8)])  7.65 us
    all_to_all x1, starting transfers between devices, on_device(): owned = exchange(chips.reshape(CHIPS, 8, W + TAIL))  7.61 us
  transfers between devices with their start and end apart: 7, of which 7 were waited for; matrix products, arithmetic and copies ran while one was open for 0% of the time, Pallas kernels for 10%

profile of v1, /device:TPU:2, one launch (start us, length us, event | category | flops | bytes accessed | tf_op | source)
XLA Modules:
  0.0 140.4 jit_solution(9862289991734038453)
XLA Ops:
  0.7 1.3 copy-done.3
  2.0 1.3 copy-done.11
  3.3 0.8 copy-done.13
  4.1 0.7 copy-done.14
  4.7 0.7 copy-done.16
  5.4 5.3 %shard_map.135 = (bf16[256,256]{1,0:T(8,128)(2,1)S(1)}, bf16[256,2560]{1,0:T(8,128)(2,1)S(1)}, bf16[256,2560]{1,0:T(8,128)(2,1)S(1)}, f32[128,2688]{1,0:T(8,128)...) custom-call(s32[1]{0:T(128)} %bitcast.core_ref, ...), custom_call_target="tpu_custom_call" | custom-call | flops 1000000000 | bytes 10000000 | tf_op jit(solution)/shard_map/pallas_call | solution.py:360
  10.7 1.1 copy-done.6
  11.8 1.1 copy-done.8
  12.8 3.3 %collective-permute-done.got_ref = f32[128,2688]{1,0:T(8,128)S(1)} collective-permute-done((f32[128,2688]{1,0:T(8,128)}, f32[128,2688]{1,0:T(8,128)S(1)}, u32[]{:S(2)}, u32[]{:S(2)}) %collective-permute-start) | collective-permute-done | bytes 1376288 | tf_op jit(solution)/shard_map/ppermute | solution.py:370
  16.2 1.8 %copy-done = f32[128,2688]{1,0:T(8,128)S(1)} copy-done((f32[128,2688]{1,0:T(8,128)S(1)}, f32[128,2688]{1,0:T(8,128)}, u32[]{:S(2)}) %copy-start) | copy-done | bytes 1376280
  18.0 1.6 %shard_map.136 = f32[128,2688]{1,0:T(8,128)} custom-call(s32[1]{0:T(128)} %bitcast.core_ref, f32[128,2688]{1,0:T(8,128)S(1)} %copy-done, f32[128,2688]{1,0:T(8,128)S(1)} %collective-permute-done.got_ref), custom_call_target="tpu_custom_call" | custom-call | flops 10000000 | bytes 4000000 | tf_op jit(solution)/shard_map/pallas_call | solution.py:371
  19.6 7.6 %all-to-all-start = ((f32[16,8,2688]{2,1,0:T(8,128)}), f32[16,8,2688]{2,1,0:T(8,128)S(1)}, u32[]{:S(2)}, u32[]{:S(2)}) async-start(f32[16,8,2688]{2,1,0:T(8,128)} %bitcast.8), calls=%async_computation | async-start | bytes 2752512 | tf_op jit(solution)/shard_map/all_to_all | solution.py:374
  27.2 1.3 copy-done.5
  28.5 1.3 copy-done.12
  29.9 13.7 %shard_map.137 = (f32[256,2560]{1,0:T(8,128)}, f32[256,256]{1,0:T(8,128)S(1)}, f32[40,256]{1,0:T(8,128)S(1)}, f32[40,256]{1,0:T(8,128)S(1)}, f32[8,128]{1,0:T(8,128)S(1)}, /*index=5*/bf16[2560,256]{1,0:T(8,128)(2,1)S(1)}) custom-call(bf16[256,2560]{1,0:T(8,128)(2,1)S(1)} %bitcast.28, bf16[256,2560]{1,0:T(8,128)(2,1)S(1)} %bitcast.22, ...), custom_call_target="tpu_custom_call" | custom-call | flops 8000000000 | bytes 10000000 | tf_op jit(solution)/shard_map/pallas_call | solution.py:375
  43.5 1.1 copy-done.10
  44.6 2.3 %all-to-all-done.in_ref = f32[16,8,2688]{2,1,0:T(8,128)S(1)} async-done(((f32[16,8,2688]{2,1,0:T(8,128)}), f32[16,8,2688]{2,1,0:T(8,128)S(1)}, u32[]{:S(2)}, u32[]{:S(2)}) %all-to-all-start) | async-done | bytes 1376288 | tf_op jit(solution)/shard_map/all_to_all | solution.py:374
  46.9 1.1 shard_map.138
  48.1 24.4 %all_to_all.15 = f32[16,8,2560]{2,1,0:T(8,128)S(1)} all-to-all(f32[16,8,2560]{2,1,0:T(8,128)S(1)} %shard_map.138), channel_id=1, replica_groups={{0,16,32,48,64,80,96,112,128,144,160,176,192,208,224,240},{8,24,40,56,7..., dimensions={0} | all-to-all | bytes 2621440 | tf_op jit(solution)/shard_map/all_to_all | solution.py:391
  72.5 2.1 %shard_map.139 = (f32[128,2560]{1,0:T(8,128)S(1)}, f32[128,2560]{1,0:T(8,128)S(1)}) custom-call(s32[1]{0:T(128)} %bitcast.core_ref, f32[128,2560]{1,0:T(8,128)S(1)} %bitcast.26, f32[128,2688]{1,0:T(8,128)S(1)} %copy-done.1, f32[128,2688]{1,0:T(8,128)} %copy-done.2), custom_call_target="tpu_custom_call" | custom-call | flops 10000000 | bytes 6000000 | tf_op jit(solution)/shard_map/pallas_call | solution.py:392
  74.9 3.0 %collective-permute-done.1.got_ref = f32[128,2560]{1,0:T(8,128)S(1)} collective-permute-done((f32[128,2560]{1,0:T(8,128)S(1)}, f32[128,2560]{1,0:T(8,128)S(1)}, u32[]{:S(2)}, u32[]{:S(2)}) %collective-permute-start.1) | collective-permute-done | bytes 1310752 | tf_op jit(solution)/shard_map/ppermute | solution.py:395
  77.9 10.7 %shard_map.140 = (bf16[256,2560]{1,0:T(8,128)(2,1)}, f32[40,256]{1,0:T(8,128)}, bf16[256,2560]{1,0:T(8,128)(2,1)}, f32[16,88,256]{2,1,0:T(8,128)}, f32[16,88,256]{2,1,0:T(8,128)}) custom-call(s32[1]{0:T(128)} %bitcast.core_ref, f32[128,2560]{1,0:T(8,128)S(1)} %get-tuple-element.34.mine_ref, f32[128,2560]{1,0:T(8,128)S(1)} %collective-permute-done.1.got_ref, ...), custom_call_target="tpu_custom_call" | custom-call | flops 3000000000 | bytes 20000000 | tf_op jit(solution)/shard_map/pallas_call | solution.py:396
  88.7 3.3 %collective-permute-done.2 = f32[16,88,256]{2,1,0:T(8,128)S(1)} collective-permute-done((f32[16,88,256]{2,1,0:T(8,128)}, f32[16,88,256]{2,1,0:T(8,128)S(1)}, u32[]{:S(2)}, u32[]{:S(2)}) %collective-permute-start.2) | collective-permute-done | bytes 1441824 | tf_op jit(solution)/shard_map/ppermute | solution.py:408
  92.1 1.5 %add.12 = f32[16,88,256]{2,1,0:T(8,128)S(1)} add(f32[16,88,256]{2,1,0:T(8,128)} %get-tuple-element.47, f32[16,88,256]{2,1,0:T(8,128)S(1)} %collective-permute-done.2) | non-fusion elementwise | flops 360448 | bytes 4325376 | tf_op jit(solution)/shard_map/add | solution.py:408
  93.6 24.6 %all_to_all.16 = f32[16,88,256]{2,1,0:T(8,128)S(1)} all-to-all(f32[16,88,256]{2,1,0:T(8,128)S(1)} %add.12), channel_id=1, replica_groups={{0,16,32,48,64,80,96,112,128,144,160,176,192,208,224,240},{8,24,40,56,7..., dimensions={0} | all-to-all | bytes 2883584 | tf_op jit(solution)/shard_map/all_to_all | solution.py:409
  118.2 2.0 %collective-permute-start.3 = (f32[88,256]{1,0:T(8,128)S(1)}, f32[88,256]{1,0:T(8,128)S(1)}, u32[]{:S(2)}, u32[]{:S(2)}) collective-permute-start(f32[88,256]{1,0:T(8,128)S(1)} %reduce_sum.9), channel_id=1, source_target_pairs={{0,1},{1,0},{2,3},{3,2},{4,5},{5,4},{6,7},{7,6},{8,9},{9,8},{10,11... | collective-permute-start | bytes 270344 | tf_op jit(solution)/shard_map/ppermute | solution.py:411
  120.3 2.6 %collective-permute-done.3 = f32[88,256]{1,0:T(8,128)S(1)} collective-permute-done((f32[88,256]{1,0:T(8,128)S(1)}, f32[88,256]{1,0:T(8,128)S(1)}, u32[]{:S(2)}, u32[]{:S(2)}) %collective-permute-start.3) | collective-permute-done | bytes 90144 | tf_op jit(solution)/shard_map/ppermute | solution.py:411
  122.9 3.4 %collective-permute-start.4 = (f32[88,256]{1,0:T(8,128)S(1)}, f32[88,256]{1,0:T(8,128)S(1)}, u32[]{:S(2)}, u32[]{:S(2)}) collective-permute-start(f32[88,256]{1,0:T(8,128)S(1)} %add.13), channel_id=1, source_target_pairs={{0,2},{1,3},{2,0},{3,1},{4,6},{5,7},{6,4},{7,5},{8,10},{9,11},{10,... | collective-permute-start | bytes 270344 | tf_op jit(solution)/shard_map/ppermute | solution.py:411
  126.2 2.5 %collective-permute-done.4 = f32[88,256]{1,0:T(8,128)S(1)} collective-permute-done((f32[88,256]{1,0:T(8,128)S(1)}, f32[88,256]{1,0:T(8,128)S(1)}, u32[]{:S(2)}, u32[]{:S(2)}) %collective-permute-start.4) | collective-permute-done | bytes 90144 | tf_op jit(solution)/shard_map/ppermute | solution.py:411
  128.8 7.9 %collective-permute-start.5 = (f32[88,256]{1,0:T(8,128)S(1)}, f32[88,256]{1,0:T(8,128)S(1)}, u32[]{:S(2)}, u32[]{:S(2)}) collective-permute-start(f32[88,256]{1,0:T(8,128)S(1)} %add.14), channel_id=1, source_target_pairs={{0,4},{1,5},{2,6},{3,7},{4,0},{5,1},{6,2},{7,3},{8,12},{9,13},{10,... | collective-permute-start | bytes 270344 | tf_op jit(solution)/shard_map/ppermute | solution.py:411
  136.7 2.6 %collective-permute-done.5 = f32[88,256]{1,0:T(8,128)S(1)} collective-permute-done((f32[88,256]{1,0:T(8,128)S(1)}, f32[88,256]{1,0:T(8,128)S(1)}, u32[]{:S(2)}, u32[]{:S(2)}) %collective-permute-start.5) | collective-permute-done | bytes 90144 | tf_op jit(solution)/shard_map/ppermute | solution.py:411
  139.8 0.6 slice.16
  (33 shorter events, 1.1 us)
Async XLA Ops:
  0.6 1.3 copy-start.3
  2.0 1.3 copy-start.11
  3.3 0.8 copy-start.13
  4.1 0.7 copy-start.14
  4.7 0.7 copy-start.16
  10.7 1.1 copy-start.6
  11.8 1.1 copy-start.8
  12.8 3.3 %collective-permute-start = (f32[128,2688]{1,0:T(8,128)}, f32[128,2688]{1,0:T(8,128)S(1)}, u32[]{:S(2)}, u32[]{:S(2)}) collective-permute-start(f32[128,2688]{1,0:T(8,128)} %get-tuple-element.29), channel_id=1, source_target_pairs={{0,8},{8,0},{16,24},{24,16},{32,40},{40,32},{48,56},{56,48},{64,72... | collective-permute-start | bytes 4128776 | tf_op jit(solution)/shard_map/ppermute | solution.py:370
  16.2 3.4 %copy-start.2 = (f32[128,2688]{1,0:T(8,128)}, f32[128,2688]{1,0:T(8,128)S(1)}, u32[]{:S(2)}) copy-start(f32[128,2688]{1,0:T(8,128)S(1)} %collective-permute-done.got_ref) | copy-start | bytes 4128772
  16.2 1.8 %copy-start = (f32[128,2688]{1,0:T(8,128)S(1)}, f32[128,2688]{1,0:T(8,128)}, u32[]{:S(2)}) copy-start(f32[128,2688]{1,0:T(8,128)} %get-tuple-element.28.keep_ref) | copy-start | bytes 4128772
  19.6 7.6 %copy-start.4 = (bf16[1,256,2560]{2,1,0:T(8,128)(2,1)S(1)}, bf16[1,256,2560]{2,1,0:T(8,128)(2,1)}, u32[]{:S(2)}) copy-start(bf16[1,256,2560]{2,1,0:T(8,128)(2,1)} %param.9) | copy-start | bytes 3932164
  19.6 27.3 %all-to-all-start = ((f32[16,8,2688]{2,1,0:T(8,128)}), f32[16,8,2688]{2,1,0:T(8,128)S(1)}, u32[]{:S(2)}, u32[]{:S(2)}) async-start(f32[16,8,2688]{2,1,0:T(8,128)} %bitcast.8), calls=%async_computation | async-start | bytes 2752512 | tf_op jit(solution)/shard_map/all_to_all | solution.py:374
  27.2 1.3 copy-start.5
  28.5 1.3 copy-start.12
  43.5 1.1 copy-start.10
  48.1 24.4 %copy-start.1 = (f32[128,2688]{1,0:T(8,128)S(1)}, f32[128,2688]{1,0:T(8,128)}, u32[]{:S(2)}) copy-start(f32[128,2688]{1,0:T(8,128)} %get-tuple-element.28.keep_ref) | copy-start | bytes 4128772
  72.5 5.5 %copy-start.7 = (bf16[256,2560]{1,0:T(8,128)(2,1)S(1)}, bf16[256,2560]{1,0:T(8,128)(2,1)}, u32[]{:S(2)}) copy-start(bf16[256,2560]{1,0:T(8,128)(2,1)} %copy-done.6) | copy-start | bytes 3932164
  72.5 5.5 %copy-start.9 = (bf16[256,2560]{1,0:T(8,128)(2,1)S(1)}, bf16[256,2560]{1,0:T(8,128)(2,1)}, u32[]{:S(2)}) copy-start(bf16[256,2560]{1,0:T(8,128)(2,1)} %copy-done.8) | copy-start | bytes 3932164
  72.5 5.5 %copy-start.15 = (f32[40]{0:T(128)S(1)}, f32[40]{0:T(128)}, u32[]{:S(2)}) copy-start(f32[40]{0:T(128)} %param.14) | copy-start | bytes 484
  72.5 5.5 %copy-start.17 = (f32[40]{0:T(128)S(1)}, f32[40]{0:T(128)}, u32[]{:S(2)}) copy-start(f32[40]{0:T(128)} %param.15) | copy-start | bytes 484
  74.6 3.3 %collective-permute-start.1 = (f32[128,2560]{1,0:T(8,128)S(1)}, f32[128,2560]{1,0:T(8,128)S(1)}, u32[]{:S(2)}, u32[]{:S(2)}) collective-permute-start(f32[128,2560]{1,0:T(8,128)S(1)} %get-tuple-element.35), channel_id=1, source_target_pairs={{0,8},{8,0},{16,24},{24,16},{32,40},{40,32},{48,56},{56,48},{64,72... | collective-permute-start | bytes 3932168 | tf_op jit(solution)/shard_map/ppermute | solution.py:395
  88.6 3.4 %collective-permute-start.2 = (f32[16,88,256]{2,1,0:T(8,128)}, f32[16,88,256]{2,1,0:T(8,128)S(1)}, u32[]{:S(2)}, u32[]{:S(2)}) collective-permute-start(f32[16,88,256]{2,1,0:T(8,128)} %get-tuple-element.48), channel_id=1, source_target_pairs={{0,8},{8,0},{16,24},{24,16},{32,40},{40,32},{48,56},{56,48},{64,72... | collective-permute-start | bytes 4325384 | tf_op jit(solution)/shard_map/ppermute | solution.py:408
  118.2 4.6 %collective-permute-start.3 = (f32[88,256]{1,0:T(8,128)S(1)}, f32[88,256]{1,0:T(8,128)S(1)}, u32[]{:S(2)}, u32[]{:S(2)}) collective-permute-start(f32[88,256]{1,0:T(8,128)S(1)} %reduce_sum.9), channel_id=1, source_target_pairs={{0,1},{1,0},{2,3},{3,2},{4,5},{5,4},{6,7},{7,6},{8,9},{9,8},{10,11... | collective-permute-start | bytes 270344 | tf_op jit(solution)/shard_map/ppermute | solution.py:411
  122.9 5.9 %collective-permute-start.4 = (f32[88,256]{1,0:T(8,128)S(1)}, f32[88,256]{1,0:T(8,128)S(1)}, u32[]{:S(2)}, u32[]{:S(2)}) collective-permute-start(f32[88,256]{1,0:T(8,128)S(1)} %add.13), channel_id=1, source_target_pairs={{0,2},{1,3},{2,0},{3,1},{4,6},{5,7},{6,4},{7,5},{8,10},{9,11},{10,... | collective-permute-start | bytes 270344 | tf_op jit(solution)/shard_map/ppermute | solution.py:411
  128.8 10.5 %collective-permute-start.5 = (f32[88,256]{1,0:T(8,128)S(1)}, f32[88,256]{1,0:T(8,128)S(1)}, u32[]{:S(2)}, u32[]{:S(2)}) collective-permute-start(f32[88,256]{1,0:T(8,128)S(1)} %add.14), channel_id=1, source_target_pairs={{0,4},{1,5},{2,6},{3,7},{4,0},{5,1},{6,2},{7,3},{8,12},{9,13},{10,... | collective-permute-start | bytes 270344 | tf_op jit(solution)/shard_map/ppermute | solution.py:411

commit v2 on v1

v2 whole, which is shorter than its diff:
```python
from functools import partial

import jax
import jax.numpy as jnp
from jax import lax
from jax.sharding import PartitionSpec as P
import jax.experimental.pallas as pl
import jax.experimental.pallas.tpu as pltpu

f32 = jnp.float32
bf16 = jnp.bfloat16

T = 256
H = 40
HD = 64
W = 2560
N = 128
HALF = 64
TAIL = 128
CHIPS = 16
ROWS = 80
PROWS = 88


def iota(shape, dim):
    return lax.broadcasted_iota(jnp.int32, shape, dim)


def split3(v):
    hi = v.astype(bf16).astype(f32)
    rest = v - hi
    mid = rest.astype(bf16).astype(f32)
    return hi, mid, rest - mid


def dot00(a, b):
    return lax.dot_general(a, b, (((0,), (0,)), ((), ())), preferred_element_type=f32)


def dot11(a, b):
    return lax.dot_general(a, b, (((1,), (1,)), ((), ())), preferred_element_type=f32)


def dot10(a, b):
    return lax.dot_general(a, b, (((1,), (0,)), ((), ())), preferred_element_type=f32)


def head_rows(count):
    lane_head = iota((count, W), 1) >> 6
    row = iota((count, W), 0)
    hit = (lane_head == row) | (lane_head == row - H) | (lane_head == row - 2 * H)
    return jnp.where(hit, 1.0, 0.0).astype(bf16)


def widen(v, spread):
    parts = jnp.concatenate(split3(v) + (jnp.zeros((8, T), f32),), axis=0).astype(bf16)
    return dot00(parts, spread)


def widen_row(row, spread):
    parts = jnp.concatenate(split3(row) + (jnp.zeros((8, 128), f32),), axis=0).astype(bf16)
    lanes = iota((N, W), 0) < H
    once = jnp.where(lanes, spread.astype(f32), 0.0).astype(bf16)
    out = dot10(parts, once)
    return out[0:8] + out[8:16] + out[16:24]


def column(row, count):
    eye = iota((count, count), 0) == iota((count, count), 1)
    return jnp.sum(jnp.where(eye, row, 0.0), axis=1, keepdims=True)


def over_positions(v, keep):
    parts = jnp.concatenate(split3(v) + (jnp.zeros((8, T), f32),), axis=0).astype(bf16)
    out = dot10(parts, jnp.where(keep, 1.0, 0.0).astype(bf16))
    return out[0:H] + out[H : 2 * H] + out[2 * H : 3 * H]


def step_sizes(logits, bias_row):
    z = logits + column(bias_row, H)
    e = jnp.exp(-jnp.abs(z))
    r = e / (2.0 + e)
    r2 = r * r
    poly = 1.0 / 17.0
    for odd in (15, 13, 11, 9, 7, 5, 3):
        poly = poly * r2 + 1.0 / odd
    dt = jnp.maximum(z, 0.0) + 2.0 * (r + r * r2 * poly)
    sig = jnp.where(z >= 0.0, 1.0, e) / (1.0 + e)
    return dt, sig


def summary_kernel(
    core_ref, bias_ref, rate_ref, logit_hbm, tok_hbm, x_hbm, g_hbm, proj_hbm,
    bc_ref, xw_ref, ge_ref, keep_ref, send_ref, more_ref, log_ref, dt_ref,
    logit_ref, tok_ref, x_ref, g_ref, proj_ref, both, sem,
):
    pairs = (
        (logit_hbm, logit_ref), (tok_hbm, tok_ref), (proj_hbm, proj_ref), (x_hbm, x_ref), (g_hbm, g_ref)
    )
    copies = [pltpu.make_async_copy(a, b, sem.at[i]) for i, (a, b) in enumerate(pairs)]
    for copy in copies:
        copy.start()
    spread = head_rows(N)
    copies[0].wait()
    dt, _ = step_sizes(logit_ref[...], bias_ref[...])
    rate = jnp.exp(column(rate_ref[...], H))
    log_decay = over_positions(-rate * dt, iota((T, T), 0) <= iota((T, T), 1))
    last = log_decay[:, T - 1 : T]
    log_ref[...] = log_decay
    dt_ref[...] = dt
    copies[1].wait()
    copies[2].wait()
    bc = dot10(tok_ref[...], proj_ref[...]).astype(bf16)
    bc_ref[...] = bc
    copies[3].wait()
    copies[4].wait()
    xw = (x_ref[...].astype(f32) * widen(jnp.exp(last - log_decay) * dt, spread)).astype(bf16)
    xw_ref[...] = xw
    ge = (g_ref[...].astype(f32) * widen(jnp.exp(log_decay), spread)).astype(bf16)
    ge_ref[...] = ge
    both[0:N, :] = dot00(bc[:, :N], xw)
    both[N : 2 * N, :] = dot00(bc[:, N:], ge)
    mine = pl.multiple_of(core_ref[0] * HALF, HALF)
    theirs = pl.multiple_of(HALF - core_ref[0] * HALF, HALF)
    keep_ref[0:HALF, 0:W] = both[pl.ds(mine, HALF), :]
    keep_ref[HALF:N, 0:W] = both[pl.ds(N + mine, HALF), :]
    send_ref[0:HALF, 0:W] = both[pl.ds(theirs, HALF), :]
    send_ref[HALF:N, 0:W] = both[pl.ds(N + theirs, HALF), :]
    more_ref[...] = both[pl.ds(pl.multiple_of(core_ref[0] * (N + HALF), HALF), HALF), :]
    on_lane = iota((H, TAIL), 0) == iota((H, TAIL), 1)
    decay = jnp.exp(jnp.sum(jnp.where(on_lane, last, 0.0), axis=0, keepdims=True))
    decay = jnp.broadcast_to(decay, (N, TAIL))
    keep_ref[:, W:] = decay
    send_ref[:, W:] = decay


def chip_kernel(core_ref, keep_ref, got_ref, out_ref):
    spread = head_rows(N)
    decay_mine = keep_ref[0:8, W:]
    decay_their = got_ref[0:8, W:]
    wide_mine = widen_row(decay_mine, spread)[0:1]
    wide_their = widen_row(decay_their, spread)[0:1]
    first = core_ref[0] == 0
    one = jnp.ones((1, W), f32)
    a = jnp.where(first, wide_their, one)
    b = jnp.where(first, one, wide_mine)
    c = jnp.where(first, one, wide_their)
    d = jnp.where(first, wide_mine, one)
    out_ref[0:HALF, 0:W] = a * keep_ref[0:HALF, 0:W] + b * got_ref[0:HALF, 0:W]
    out_ref[HALF:N, 0:W] = c * keep_ref[HALF:N, 0:W] + d * got_ref[HALF:N, 0:W]
    out_ref[:, W:] = keep_ref[:, W:] * got_ref[:, W:]


def scan_kernel(back_ref, in_ref, after_ref, out_ref, wide):
    spread = head_rows(N)
    for c in range(CHIPS):
        wide[c] = widen_row(in_ref[c, :, W:], spread)
    back = back_ref[0]
    state = jnp.zeros((8, W), f32)
    for i in range(CHIPS):
        c = jnp.where(back == 1, CHIPS - 1 - i, i)
        out_ref[c] = state
        state = wide[c] * state + in_ref[c, :, 0:W]


def within_kernel(
    first, x_ref, g_ref, bc_ref, log_ref, dt_ref, before_ref,
    du_ref, sg_ref, cross_ref, col_ref,
    wide_log, late_log, ds, rows,
):
    half = T // 2
    spread = head_rows(N)
    log_decay = log_ref[...]
    dt = dt_ref[...]
    wide_log[...] = widen(log_decay, spread)
    late_log[...] = log_decay - jnp.log(dt)
    b = bc_ref[:, :N]
    c = bc_ref[:, N:]
    scores = dot11(c, b)
    ds[...] = jnp.zeros((T, T), f32)
    rows[...] = jnp.zeros((T, 128), f32)
    col_ref[...] = jnp.zeros((H, T), f32)
    causal = iota((half, half), 0) >= iota((half, half), 1)
    lane = iota((T, 128), 1)

    def pair(i, carry):
        cols = pl.ds(pl.multiple_of((first + i) * 128, 128), 128)
        xp = x_ref[:, cols]
        gp = g_ref[:, cols]
        logs = wide_log[:, cols]
        total = jnp.zeros((T, 128), f32)
        for m in range(2):
            h = 2 * (first + i) + m
            gm = jnp.where((lane >= HD) == (m == 1), gp.astype(f32), 0.0).astype(bf16)
            q0 = dot11(gm[0:half], xp[0:half])
            q1 = dot11(gm[half:], xp)
            late = late_log[pl.ds(h, 1), :]
            lc = logs[:, m * HD : m * HD + 1]
            gap0 = lc[0:half] - late[:, 0:half]
            gap1 = lc[half:] - late[:, half:]
            dec0 = jnp.exp(jnp.where(causal, gap0, -1e30))
            dec1 = jnp.concatenate(
                [
                    jnp.exp(lc[half:] - late[:, 0:half]),
                    jnp.exp(jnp.where(causal, gap1, -1e30)),
                ],
                axis=1,
            )
            m0 = dec0 * scores[0:half, 0:half]
            m1 = dec1 * scores[half:, :]
            ds[0:half, 0:half] += dec0 * q0
            ds[half:, :] += dec1 * q1
            p0 = m0 * q0
            p1 = m1 * q1
            rsum = jnp.concatenate(
                [jnp.sum(p0, axis=1, keepdims=True), jnp.sum(p1, axis=1, keepdims=True)], axis=0
            )
            rows[...] += jnp.where(lane == h, rsum, 0.0)
            csum1 = jnp.sum(p1, axis=0, keepdims=True)
            csum0 = jnp.sum(p0, axis=0, keepdims=True)
            col_ref[pl.ds(h, 1), :] = csum1 + jnp.concatenate(
                [csum0, jnp.zeros((1, half), f32)], axis=1
            )
            early = dot00(m0.astype(bf16), gm[0:half])
            late_part = dot00(m1.astype(bf16), gm[half:])
            total = total + late_part + jnp.concatenate(
                [early, jnp.zeros((half, 128), f32)], axis=0
            )
        du_ref[:, pl.ds(pl.multiple_of(i * 128, 128), 128)] = total
        return carry

    lax.fori_loop(0, H // 4, pair, 0)
    hi, mid, _ = split3(ds[...])
    hi = hi.astype(bf16)
    mid = mid.astype(bf16)
    sg_ref[:, :N] = before_ref[:, :N] + dot00(hi, c) + dot00(mid, c)
    sg_ref[:, N:] = before_ref[:, N:] + dot10(hi, b) + dot10(mid, b)
    cross_ref[...] = rows[...].T[0:H, :] - col_ref[...]


def token_kernel(
    core_ref, tok_ref, x_ref, g_ref, logit_ref, bias_ref,
    keep_ref, send_ref, sig_ref, skip_ref, turned,
):
    spread = head_rows(N)
    turned[...] = tok_ref[...].T
    for chip in range(CHIPS):
        mine = pl.multiple_of((2 * chip + core_ref[0]) * ROWS, 16)
        theirs = pl.multiple_of((2 * chip + 1 - core_ref[0]) * ROWS, 16)
        keep_ref[chip * ROWS : (chip + 1) * ROWS, :] = turned[pl.ds(mine, ROWS), :]
        send_ref[chip * ROWS : (chip + 1) * ROWS, :] = turned[pl.ds(theirs, ROWS), :].astype(f32)
    x = x_ref[...].astype(f32)
    g = g_ref[...].astype(f32)
    _, sig_ref[...] = step_sizes(logit_ref[...], bias_ref[...])
    part = jnp.sum((x * g).reshape(T // 8, 8, W), axis=0)
    skip = dot11(jnp.concatenate(split3(part), axis=0).astype(bf16), spread)
    skip = jnp.sum(skip, axis=0, keepdims=True)
    skip_ref[...] = jnp.broadcast_to(jnp.where(iota((1, 128), 1) < H, skip, 0.0), (8, 128))


def half_states(first, decay, chip_ref, extra):
    one = jnp.ones((1, W), f32)
    zero = jnp.zeros((1, W), f32)
    s = jnp.where(first, one, decay) * chip_ref[0:HALF, :] + jnp.where(first, zero, one) * extra
    e = jnp.where(first, decay, one) * chip_ref[HALF:N, :] + jnp.where(first, one, zero) * extra
    return s, e, jnp.sum((s * e).reshape(HALF // 8, 8, W), axis=0)


def near_kernel(core_ref, chip_ref, got_ref, xw_ref, ge_ref, s_ref, e_ref, meet_ref, part_ref, decay_ref):
    first = core_ref[0] == 0
    wide = widen_row(got_ref[0:8, W:], head_rows(N))[0:1]
    extra = jnp.where(first, got_ref[HALF:N, 0:W], got_ref[0:HALF, 0:W])
    decay_ref[...] = got_ref[0:8, W:]
    s, e, meet_ref[...] = half_states(first, wide, chip_ref, extra)
    s_ref[...] = s.astype(bf16)
    e_ref[...] = e.astype(bf16)
    part_ref[...] = jnp.concatenate(
        [dot11(xw_ref[...], e_ref[...]), dot11(ge_ref[...], s_ref[...])], axis=1
    )


def state_kernel(
    core_ref, chip_ref, more_ref, near_s_ref, near_e_ref, near_meet_ref, part_ref, decay_ref,
    xw_ref, ge_ref, sgin_ref,
    sg_ref, sgsend_ref, s_ref, e_ref, meet_ref,
):
    core = core_ref[0]
    first = core == 0
    wide = widen_row(decay_ref[...], head_rows(N))[0:1]
    s, e, meet = half_states(first, wide, chip_ref, more_ref[...])
    meet_ref[...] = near_meet_ref[...] + meet
    s = s.astype(bf16)
    e = e.astype(bf16)
    own = pl.ds(pl.multiple_of(core * HALF, HALF), HALF)
    other = pl.ds(pl.multiple_of(HALF - core * HALF, HALF), HALF)
    s_ref[own, :] = near_s_ref[...]
    e_ref[own, :] = near_e_ref[...]
    s_ref[other, :] = s
    e_ref[other, :] = e
    far = jnp.concatenate([dot11(xw_ref[...], e), dot11(ge_ref[...], s)], axis=1)
    near = part_ref[...]
    lo = jnp.where(first, near, far)
    hi = jnp.where(first, far, near)
    sg = sgin_ref[...] + jnp.concatenate(
        [lo[:, :HALF], hi[:, :HALF], lo[:, HALF:], hi[:, HALF:]], axis=1
    )
    sg = sg.astype(bf16)
    sg_ref[...] = sg
    sgsend_ref[...] = sg.astype(f32)


def own_weight_kernel(keep_ref, sg_ref, out_ref):
    out_ref[...] = dot10(keep_ref[...], sg_ref[...])


def weight_kernel(own_ref, got_ref, sggot_ref, param_ref, paramgot_ref, out_ref):
    out = own_ref[...] + dot10(got_ref[...].astype(bf16), sggot_ref[...].astype(bf16))
    out_ref[:, 0:ROWS, :] = out.reshape(CHIPS, ROWS, 2 * N)
    params = param_ref[...] + paramgot_ref[...]
    params = jnp.concatenate([params, jnp.zeros_like(params)], axis=1)
    out_ref[:, ROWS:PROWS, :] = jnp.broadcast_to(params[None], (CHIPS, 8, 2 * N))


def logit_kernel(
    s_ref, e_ref, meet_ref, xw_ref, ge_ref, bc_ref, log_ref, dt_ref, sig_ref, rate_ref,
    crossa_ref, crossb_ref, cola_ref, colb_ref, skip_ref,
    logit_ref, param_ref,
):
    spread = head_rows(N)
    b = bc_ref[:, :N]
    c = bc_ref[:, N:]
    log_decay = log_ref[...]
    dt = dt_ref[...]
    last = log_decay[:, T - 1 : T]
    pick = spread[0:48]
    eb = dot10(b, e_ref[...])
    v = dot11(pick, (xw_ref[...].astype(f32) * eb).astype(bf16))[0:H]
    from_start = dot10(c, s_ref[...])
    carry = dot11(pick, (ge_ref[...].astype(f32) * from_start).astype(bf16))[0:H]
    meet = dot11(pick, jnp.concatenate(split3(meet_ref[...]), axis=0).astype(bf16))[0:H]
    through = jnp.sum(meet, axis=1, keepdims=True) * jnp.exp(last)
    row = iota((T, T), 0)
    col = iota((T, T), 1)
    log_grad = (
        through
        + over_positions(carry + crossa_ref[...] + crossb_ref[...], row >= col)
        + over_positions(v, row < col)
    )
    rate = jnp.exp(column(rate_ref[...], H))
    dt_grad = (cola_ref[...] + colb_ref[...] + v) / dt - rate * log_grad
    logit = dt_grad * sig_ref[...]
    logit_ref[...] = logit
    on_lane = iota((H, 128), 0) == iota((H, 128), 1)

    def as_row(colsum):
        return jnp.sum(jnp.where(on_lane, colsum, 0.0), axis=0, keepdims=True)

    rate_row = as_row(jnp.sum(-rate * dt * log_grad, axis=1, keepdims=True))
    bias_row = as_row(jnp.sum(logit, axis=1, keepdims=True))
    param_ref[...] = jnp.concatenate(
        [rate_row, bias_row, skip_ref[0:1, :], jnp.zeros((5, 128), f32)], axis=0
    )


def scan_grad_kernel(
    e_ref, g_ref, bc_ref, log_ref, dt_ref, direct_ref, dua_ref, dub_ref, scan_ref
):
    spread = head_rows(N)
    log_decay = log_ref[...]
    eb = dot10(bc_ref[:, :N], e_ref[...])
    to_end = widen(jnp.exp(log_decay[:, T - 1 : T] - log_decay) * dt_ref[...], spread)
    direct_row = jnp.broadcast_to(
        jnp.concatenate([direct_ref[...], jnp.zeros((1, 128 - H), f32)], axis=1), (8, 128)
    )
    direct = widen_row(direct_row, spread)[0:1]
    half = W // 2
    for at, ref in ((0, dua_ref), (half, dub_ref)):
        to = slice(at, at + half)
        scan_ref[:, to] = (
            ref[...] + to_end[:, to] * eb[:, to] + direct[:, to] * g_ref[:, to].astype(f32)
        ).astype(bf16)


def mixer_kernel(sg_ref, proj_ref, mixer_ref):
    mixer_ref[...] = dot11(sg_ref[...], proj_ref[...]).astype(bf16)


def call(kernel, outs, scratch=(), smem=1, far=0, flops=0, moved=0, n_in=0, mib=32):
    vmem = pl.BlockSpec(memory_space=pltpu.VMEM)
    return pl.pallas_call(
        kernel,
        out_shape=[jax.ShapeDtypeStruct(s, d) for s, d in outs],
        in_specs=[pl.BlockSpec(memory_space=pltpu.SMEM)] * smem
        + [vmem] * n_in
        + [pl.BlockSpec(memory_space=pltpu.HBM)] * far,
        out_specs=[vmem] * len(outs),
        scratch_shapes=list(scratch),
        compiler_params=pltpu.CompilerParams(vmem_limit_bytes=mib * 1024 * 1024),
        cost_estimate=pl.CostEstimate(flops=flops, bytes_accessed=moved, transcendentals=0),
    )


def on_device(tokens, scan_input, logits, grads, proj, bias, rate_log, direct):
    tok, x, lg, g = tokens[0], scan_input[0], logits[0], grads[0]
    place = lax.axis_index("seq")
    core = lax.rem(place, 2).astype(jnp.int32).reshape(1)
    chip = lax.div(place, 2)
    back = (chip >= CHIPS // 2).astype(jnp.int32).reshape(1)
    bias_row = bias.reshape(1, H)
    rate_row = rate_log.reshape(1, H)
    direct_row = direct.reshape(1, H)
    swap = [(i, i ^ 1) for i in range(2 * CHIPS)]
    same_core = [[2 * i + k for i in range(CHIPS)] for k in range(2)]
    exchange = partial(
        lax.all_to_all, axis_name="seq", split_axis=0, concat_axis=0, axis_index_groups=same_core
    )

    bc, xw, ge, keep, send, more, log_decay, dt = call(
        summary_kernel,
        [
            ((T, 2 * N), bf16), ((T, W), bf16), ((T, W), bf16),
            ((N, W + TAIL), f32), ((N, W + TAIL), f32), ((HALF, W), f32),
            ((H, T), f32), ((H, T), f32),
        ],
        [
            pltpu.VMEM((H, T), f32), pltpu.VMEM((T, W), bf16), pltpu.VMEM((T, W), bf16),
            pltpu.VMEM((T, W), bf16), pltpu.VMEM((W, 2 * N), bf16), pltpu.VMEM((2 * N, W), f32),
            pltpu.SemaphoreType.DMA((5,)),
        ],
        n_in=2, far=5, flops=int(1e9), moved=int(1e7), mib=50,
    )(core, bias_row, rate_row, lg, tok, x, g, proj)
    got = lax.ppermute(send, "seq", swap)
    (chips,) = call(
        chip_kernel, [((N, W + TAIL), f32)], n_in=2, flops=int(1e7), moved=int(4e6), mib=8
    )(core, keep, got)
    chips, tok_b = lax.optimization_barrier((chips, tok))
    owned = exchange(chips.reshape(CHIPS, 8, W + TAIL))

    def within(first, dt, before):
        return call(
            partial(within_kernel, first),
            [((T, W // 2), f32), ((T, 2 * N), f32), ((H, T), f32), ((H, T), f32)],
            [
                pltpu.VMEM((T, W), f32), pltpu.VMEM((H, T), f32),
                pltpu.VMEM((T, T), f32), pltpu.VMEM((T, 128), f32),
            ],
            smem=0, n_in=6, flops=int(8e9), moved=int(5e6), mib=56,
        )(x, g, bc, log_decay, dt, before)

    du_a, sg_a, cross_a, col_a = within(0, dt, jnp.zeros((T, 2 * N), f32))
    tokt, tokt_send, sig, skip = call(
        token_kernel,
        [
            ((W // 2, T), bf16), ((W // 2, T), f32), ((H, T), f32), ((8, 128), f32),
        ],
        [pltpu.VMEM((W, T), bf16)],
        n_in=5, flops=int(3e9), moved=int(8e6), mib=56,
    )(core, tok_b, x, g, lg, bias_row)
    tokt_got = lax.ppermute(tokt_send, "seq", swap)
    more = lax.ppermute(more, "seq", swap)
    (starts,) = call(
        scan_kernel, [((CHIPS, 8, W), f32)], [pltpu.VMEM((CHIPS, 8, W), f32)],
        n_in=2, flops=int(1e7), moved=int(3e6), mib=6,
    )(back, owned, col_a)
    returned = exchange(starts).reshape(N, W)
    _, more, tokt_got, dt_b = lax.optimization_barrier((starts, more, tokt_got, dt))
    du_b, sg_b, cross_b, col_b = within(H // 4, dt_b, sg_a)
    returned, sg_b = lax.optimization_barrier((returned, sg_b))
    returned_got = lax.ppermute(returned, "seq", swap)
    near_s, near_e, near_meet, near_part, decay = call(
        near_kernel,
        [((HALF, W), bf16), ((HALF, W), bf16), ((8, W), f32), ((T, N), f32), ((8, TAIL), f32)],
        n_in=4, flops=int(4e8), moved=int(6e6), mib=10,
    )(core, returned, got, xw, ge)
    sg, sg_send, s_all, e_all, meet = call(
        state_kernel,
        [
            ((T, 2 * N), bf16), ((T, 2 * N), f32), ((N, W), bf16), ((N, W), bf16), ((8, W), f32)
        ],
        n_in=10, flops=int(4e8), moved=int(6e6), mib=10,
    )(
        core, returned_got, more, near_s, near_e, near_meet, near_part, decay, xw, ge, sg_b
    )
    sg_got = lax.ppermute(sg_send, "seq", swap)
    logit_grad, params = call(
        logit_kernel, [((H, T), f32), ((8, 128), f32)], smem=0, n_in=15,
        flops=int(4e8), moved=int(4e6), mib=10,
    )(
        s_all, e_all, meet, xw, ge, bc, log_decay, dt, sig, rate_row,
        cross_a, cross_b, col_a, col_b, skip,
    )
    params_got = lax.ppermute(params, "seq", swap)
    (own_weights,) = call(
        own_weight_kernel, [((W // 2, 2 * N), f32)], smem=0, n_in=2,
        flops=int(2e8), moved=int(2e6), mib=6,
    )(tokt, sg)
    (weights,) = call(
        weight_kernel, [((CHIPS, PROWS, 2 * N), f32)], smem=0, n_in=5,
        flops=int(2e8), moved=int(4e6), mib=8,
    )(own_weights, tokt_got, sg_got, params, params_got)
    parts = exchange(weights)
    parts, e_late, sg_late = lax.optimization_barrier((parts, e_all, sg))
    (scan_grad,) = call(
        scan_grad_kernel, [((T, W), bf16)], smem=0, n_in=8, flops=int(2e9), moved=int(1e7), mib=56,
    )(e_late, g, bc, log_decay, dt, direct_row, du_a, du_b)
    (mixer_grad,) = call(
        mixer_kernel, [((T, W), bf16)], smem=0, n_in=2, flops=int(1e9), moved=int(3e6), mib=56,
    )(sg_late, proj)
    total = jnp.sum(parts, axis=0)
    for k in (1, 2, 4):
        total = total + lax.ppermute(total, "dp", [(i, i ^ k) for i in range(8)])
    total = total * (float(T * 2 * CHIPS * 8) ** -0.5)
    return (
        scan_grad[None],
        logit_grad[None],
        mixer_grad[None],
        total[0:ROWS],
        total[ROWS, 0:H],
        total[ROWS + 2, 0:H],
        total[ROWS + 1, 0:H],
    )


def solution(mesh):
    placed = (
        P("dp", "seq", None),
        P("dp", "seq", None),
        P("dp", None, "seq"),
        P("dp", "seq", None),
        P(),
        P(),
        P(),
        P(),
    )
    return jax.shard_map(
        on_device,
        mesh=mesh,
        in_specs=placed,
        out_specs=(
            P("dp", "seq", None),
            P("dp", None, "seq"),
            P("dp", "seq", None),
            P("seq", None),
            P(),
            P(),
            P(),
        ),
        check_vma=False,
    )
```

time: 142 us -> 133 us (0.937)
  blocking collectives: 48.9 us -> 25.1 us
  Pallas kernels: 34.5 us -> 48.2 us
  starting transfers between devices: 21.3 us -> 26.6 us
  local copies, waits for them, and re-layouts: 13.6 us -> 10.2 us
  waiting for transfers between devices: 19.6 us -> 21.2 us
  other arithmetic: 1.68 us -> 0.13 us
    all_to_all x2 -> x1, blocking collectives: 48.9 us -> 25.1 us  [on_device(): parts = exchange(weights)]
    pallas_call x3 -> x10, Pallas kernels: 26.5 us -> 39.1 us  [the longest x2 18.8 us: within(): call(partial(within_kernel, first), [((T, W // 2), f32), ((T, 2 * N), f32...]
    all_to_all x0 -> x1, waiting for transfers between devices: none -> 8.35 us  [on_device(): returned = exchange(starts).reshape(N, W)]
    all_to_all x0 -> x1, starting transfers between devices: none -> 6.97 us  [on_device(): returned = exchange(starts).reshape(N, W)]
    ppermute x2 -> x5, waiting for transfers between devices: 6.34 us -> 0.8 us  [the longest x1 0.79 us: on_device(): params_got = lax.ppermute(params, 'seq', swap)]
    unnamed x36 -> x52, local copies, waits for them, and re-layouts: 12.4 us -> 8.27 us
    ppermute x3, waiting for transfers between devices: 7.65 us -> 3.61 us  [on_device(): total = total + lax.ppermute(total, 'dp', [(i, i ^ k) for i in range(8)])]
    all_to_all x1, waiting for transfers between devices: 2.32 us -> 5.11 us  [on_device(): owned = exchange(chips.reshape(CHIPS, 8, W + TAIL))]
  transfers between devices with their start and end apart: 7 -> 11, of which waited for: 7 -> 6; matrix products, arithmetic and copies ran while one was open for 0% -> 1% of each run, Pallas kernels for 10% -> 29%
where the time goes in v2:
time: 133 us; the launch traced here: 132 us
  Pallas kernels  48.2 us (36%)
  starting transfers between devices  26.6 us (20%)
  blocking collectives  25.1 us (19%)
  waiting for transfers between devices  21.2 us (16%)
  local copies, waits for them, and re-layouts  10.2 us (8%)
    all_to_all x1, blocking collectives, on_device(): parts = exchange(weights)  25.1 us
    pallas_call x2, Pallas kernels, within(): call(partial(within_kernel, first), [((T, W // 2), f32), ((T, 2 * N), f32...  18.8 us
    ppermute x3, starting transfers between devices, on_device(): total = total + lax.ppermute(total, 'dp', [(i, i ^ k) for i in range(8)])  10.9 us
    all_to_all x1, waiting for transfers between devices, on_device(): returned = exchange(starts).reshape(N, W)  8.35 us
    unnamed x52, local copies, waits for them, and re-layouts  8.27 us
    all_to_all x1, starting transfers between devices, on_device(): owned = exchange(chips.reshape(CHIPS, 8, W + TAIL))  7.48 us
    all_to_all x1, starting transfers between devices, on_device(): returned = exchange(starts).reshape(N, W)  6.97 us
    pallas_call x1, Pallas kernels, on_device(): call(summary_kernel, [((T, 2 * N), bf16), ((T, W), bf16), ((T, W), bf16),...  6.15 us
  transfers between devices with their start and end apart: 11, of which 6 were waited for; matrix products, arithmetic and copies ran while one was open for 1% of the time, Pallas kernels for 29%

profile of v2, /device:TPU:2, one launch (start us, length us, event | category | flops | bytes accessed | tf_op | source)
XLA Modules:
  0.0 132.3 jit_solution(15882653700588265146)
XLA Ops:
  0.6 0.8 copy-done.13
  1.4 0.7 copy-done.23
  2.1 0.7 copy-done.25
  2.7 6.2 %shard_map.135 = (bf16[256,256]{1,0:T(8,128)(2,1)S(1)}, bf16[256,2560]{1,0:T(8,128)(2,1)S(1)}, bf16[256,2560]{1,0:T(8,128)(2,1)S(1)}, f32[128,2688]{1,0:T(8,128)...) custom-call(s32[1]{0:T(128)} %bitcast.core_ref, ...), custom_call_target="tpu_custom_call" | custom-call | flops 1000000000 | bytes 10000000 | tf_op jit(solution)/shard_map/pallas_call | solution.py:418
  9.0 3.3 %collective-permute-done.got_ref = f32[128,2688]{1,0:T(8,128)S(1)} collective-permute-done((f32[128,2688]{1,0:T(8,128)}, f32[128,2688]{1,0:T(8,128)S(1)}, u32[]{:S(2)}, u32[]{:S(2)}) %collective-permute-start) | collective-permute-done | bytes 1376288 | tf_op jit(solution)/shard_map/ppermute | solution.py:432
  12.4 1.8 %copy-done.4 = f32[128,2688]{1,0:T(8,128)S(1)} copy-done((f32[128,2688]{1,0:T(8,128)S(1)}, f32[128,2688]{1,0:T(8,128)}, u32[]{:S(2)}) %copy-start.4) | copy-done | bytes 1376280
  14.7 1.1 copy-done.2
  15.8 7.5 %all-to-all-start = ((f32[16,8,2688]{2,1,0:T(8,128)}), f32[16,8,2688]{2,1,0:T(8,128)}, u32[]{:S(2)}, u32[]{:S(2)}) async-start(f32[16,8,2688]{2,1,0:T(8,128)} %bitcast.20), calls=%async_computation | async-start | bytes 2752512 | tf_op jit(solution)/shard_map/all_to_all | solution.py:437
  23.3 4.1 %shard_map.137 = (bf16[1280,256]{1,0:T(8,128)(2,1)}, f32[1280,256]{1,0:T(8,128)}, f32[40,256]{1,0:T(8,128)}, f32[8,128]{1,0:T(8,128)}) custom-call(s32[1]{0:T(128)} %bitcast.core_ref, bf16[256,2560]{1,0:T(8,128)(2,1)} %bitcast.28, bf16[256,2560]{1,0:T(8,128)(2,1)} %bitcast.30, bf16[256,2560]{1,0:T(8,128)(2,1)} %bitcast.34, f32[40,256]{1,0:T(8,128)} %bitcast.21, ...), custom_call_target="tpu_custom_call" | custom-call | flops 3000000000 | bytes 8000000 | tf_op jit(solution)/shard_map/pallas_call | solution.py:451
  27.9 0.7 broadcast_in_dim.12.before_ref
  28.6 9.4 %shard_map.138 = (f32[256,1280]{1,0:T(8,128)}, f32[256,256]{1,0:T(8,128)}, f32[40,256]{1,0:T(8,128)}, f32[40,256]{1,0:T(8,128)}) custom-call(bf16[256,2560]{1,0:T(8,128)(2,1)} %bitcast.31, bf16[256,2560]{1,0:T(8,128)(2,1)} %bitcast.35, bf16[256,256]{1,0:T(8,128)(2,1)} %copy-done.10, f32[40,256]{1,0:T(8,128)} %copy-done.14, f32[40,256]{1,0:T(8,128)} %copy-done.16, ...), custom_call_target="tpu_custom_call" | custom-call | flops 8000000000 | bytes 5000000 | tf_op jit(solution)/shard_map/pallas_call | solution.py:440
  38.0 5.1 %all-to-all-done.in_ref = f32[16,8,2688]{2,1,0:T(8,128)} async-done(((f32[16,8,2688]{2,1,0:T(8,128)}), f32[16,8,2688]{2,1,0:T(8,128)}, u32[]{:S(2)}, u32[]{:S(2)}) %all-to-all-start) | async-done | bytes 1376288 | tf_op jit(solution)/shard_map/all_to_all | solution.py:437
  43.1 0.8 copy-done.8
  43.9 2.5 %shard_map.139 = f32[16,8,2560]{2,1,0:T(8,128)S(1)} custom-call(s32[1]{0:T(128)} %bitcast.7.back_ref, f32[16,8,2688]{2,1,0:T(8,128)} %all-to-all-done.in_ref, f32[40,256]{1,0:T(8,128)S(1)} %copy-done.8), custom_call_target="tpu_custom_call" | custom-call | flops 10000000 | bytes 3000000 | tf_op jit(solution)/shard_map/pallas_call | solution.py:461
  46.4 1.0 copy-done.3
  47.4 7.0 %all-to-all-start.1 = ((f32[16,8,2560]{2,1,0:T(8,128)}), f32[16,8,2560]{2,1,0:T(8,128)}, u32[]{:S(2)}, u32[]{:S(2)}) async-start(f32[16,8,2560]{2,1,0:T(8,128)} %copy-done.3), calls=%async_computation.1 | async-start | bytes 2621440 | tf_op jit(solution)/shard_map/all_to_all | solution.py:465
  54.4 9.4 %shard_map.140 = (f32[256,1280]{1,0:T(8,128)}, f32[256,256]{1,0:T(8,128)}, f32[40,256]{1,0:T(8,128)}, f32[40,256]{1,0:T(8,128)}) custom-call(bf16[256,2560]{1,0:T(8,128)(2,1)} %bitcast.32, bf16[256,2560]{1,0:T(8,128)(2,1)} %bitcast.36, bf16[256,256]{1,0:T(8,128)(2,1)} %copy-done.10, f32[40,256]{1,0:T(8,128)} %copy-done.14, f32[40,256]{1,0:T(8,128)} %copy-done.16, ...), custom_call_target="tpu_custom_call" | custom-call | flops 8000000000 | bytes 5000000 | tf_op jit(solution)/shard_map/pallas_call | solution.py:440
  63.8 8.3 %all-to-all-done.1 = f32[16,8,2560]{2,1,0:T(8,128)} async-done(((f32[16,8,2560]{2,1,0:T(8,128)}), f32[16,8,2560]{2,1,0:T(8,128)}, u32[]{:S(2)}, u32[]{:S(2)}) %all-to-all-start.1) | async-done | bytes 1310752 | tf_op jit(solution)/shard_map/all_to_all | solution.py:465
  72.2 1.3 %copy-done.1 = f32[128,2688]{1,0:T(8,128)S(1)} copy-done((f32[128,2688]{1,0:T(8,128)S(1)}, f32[128,2688]{1,0:T(8,128)}, u32[]{:S(2)}) %copy-start.1) | copy-done | bytes 1376280
  73.5 2.4 %shard_map.141 = (bf16[64,2560]{1,0:T(8,128)(2,1)S(1)}, bf16[64,2560]{1,0:T(8,128)(2,1)S(1)}, f32[8,2560]{1,0:T(8,128)S(1)}, f32[256,128]{1,0:T(8,128)S(1)}, f32[8,128]{1,0:T(8,128)S(1)}) custom-call(s32[1]{0:T(128)} %bitcast.core_ref, f32[128,2560]{1,0:T(8,128)} %bitcast.9.chip_ref, f32[128,2688]{1,0:T(8,128)S(1)} %copy-done.1, ...), custom_call_target="tpu_custom_call" | custom-call | flops 400000000 | bytes 6000000 | tf_op jit(solution)/shard_map/pallas_call | solution.py:470
  76.1 1.1 shard_map.142
  77.9 2.5 %shard_map.144 = (f32[40,256]{1,0:T(8,128)}, f32[8,128]{1,0:T(8,128)S(1)}) custom-call(bf16[128,2560]{1,0:T(8,128)(2,1)S(1)} %get-tuple-element.76.s_ref, bf16[128,2560]{1,0:T(8,128)(2,1)S(1)} %get-tuple-element.85.e_ref, f32[8,2560]{1,0:T(8,128)S(1)} %get-tuple-element.78.meet_ref, bf16[256,2560]{1,0:T(8,128)(2,1)S(1)} %get-tuple-element.65.xw_ref, ...), custom_call_target="tpu_custom_call" | custom-call | flops 400000000 | bytes 4000000 | tf_op jit(solution)/shard_map/pallas_call | solution.py:485
  80.8 0.8 collective-permute-done.5.paramgot_ref
  81.6 1.7 %shard_map.145 = f32[16,88,256]{2,1,0:T(8,128)S(1)} custom-call(f32[1280,256]{1,0:T(8,128)S(1)} %shard_map.143.own_ref, f32[1280,256]{1,0:T(8,128)} %collective-permute-done.2.got_ref, f32[256,256]{1,0:T(8,128)S(1)} %collective-permute-done.4.sggot_ref, f32[8,128]{1,0:T(8,128)S(1)} %get-tuple-element.84.param_ref, ...), custom_call_target="tpu_custom_call" | custom-call | flops 200000000 | bytes 4000000 | tf_op jit(solution)/shard_map/pallas_call | solution.py:497
  83.3 25.1 %all_to_all.15 = f32[16,88,256]{2,1,0:T(8,128)S(1)} all-to-all(f32[16,88,256]{2,1,0:T(8,128)S(1)} %shard_map.145), channel_id=1, replica_groups={{0,16,32,48,64,80,96,112,128,144,160,176,192,208,224,240},{8,24,40,56,7..., dimensions={0} | all-to-all | bytes 2883584 | tf_op jit(solution)/shard_map/all_to_all | solution.py:501
  108.5 2.0 %collective-permute-start.6 = (f32[88,256]{1,0:T(8,128)S(1)}, f32[88,256]{1,0:T(8,128)S(1)}, u32[]{:S(2)}, u32[]{:S(2)}) collective-permute-start(f32[88,256]{1,0:T(8,128)S(1)} %reduce_sum.9), channel_id=1, source_target_pairs={{0,1},{1,0},{2,3},{3,2},{4,5},{5,4},{6,7},{7,6},{8,9},{9,8},{10,11... | collective-permute-start | bytes 270344 | tf_op jit(solution)/shard_map/ppermute | solution.py:511
  110.5 2.6 %collective-permute-done.6 = f32[88,256]{1,0:T(8,128)S(1)} collective-permute-done((f32[88,256]{1,0:T(8,128)S(1)}, f32[88,256]{1,0:T(8,128)S(1)}, u32[]{:S(2)}, u32[]{:S(2)}) %collective-permute-start.6) | collective-permute-done | bytes 90144 | tf_op jit(solution)/shard_map/ppermute | solution.py:511
  113.1 3.4 %collective-permute-start.7 = (f32[88,256]{1,0:T(8,128)S(1)}, f32[88,256]{1,0:T(8,128)S(1)}, u32[]{:S(2)}, u32[]{:S(2)}) collective-permute-start(f32[88,256]{1,0:T(8,128)S(1)} %add.9), channel_id=1, source_target_pairs={{0,2},{1,3},{2,0},{3,1},{4,6},{5,7},{6,4},{7,5},{8,10},{9,11},{10,... | collective-permute-start | bytes 270344 | tf_op jit(solution)/shard_map/ppermute | solution.py:511
  116.5 5.1 %shard_map.146 = bf16[256,2560]{1,0:T(8,128)(2,1)} custom-call(bf16[128,2560]{1,0:T(8,128)(2,1)} %copy-done.6, bf16[256,2560]{1,0:T(8,128)(2,1)} %bitcast.37, bf16[256,256]{1,0:T(8,128)(2,1)} %copy-done.10, f32[40,256]{1,0:T(8,128)} %copy-done.14, f32[40,256]{1,0:T(8,128)} %copy-done.16, f32[1,40]{1,0:T(1,128)} %bitcast.39, ...), custom_call_target="tpu_custom_call" | custom-call | flops 2000000000 | bytes 10000000 | tf_op jit(solution)/shard_map/pallas_call | solution.py:503
  121.6 5.5 %collective-permute-start.8 = (f32[88,256]{1,0:T(8,128)S(1)}, f32[88,256]{1,0:T(8,128)S(1)}, u32[]{:S(2)}, u32[]{:S(2)}) collective-permute-start(f32[88,256]{1,0:T(8,128)S(1)} %add.10), channel_id=1, source_target_pairs={{0,4},{1,5},{2,6},{3,7},{4,0},{5,1},{6,2},{7,3},{8,12},{9,13},{10,... | collective-permute-start | bytes 270344 | tf_op jit(solution)/shard_map/ppermute | solution.py:511
  127.2 3.0 %shard_map.147 = bf16[256,2560]{1,0:T(8,128)(2,1)} custom-call(bf16[256,256]{1,0:T(8,128)(2,1)} %copy-done.12, bf16[2560,256]{1,0:T(8,128)(2,1)} %proj_ref.1), custom_call_target="tpu_custom_call" | custom-call | flops 1000000000 | bytes 3000000 | tf_op jit(solution)/shard_map/pallas_call | solution.py:506
  130.1 1.0 collective-permute-done.8
  (63 shorter events, 3.5 us)
Async XLA Ops:
  8.9 5.8 %copy-start.10 = (bf16[256,256]{1,0:T(8,128)(2,1)}, bf16[256,256]{1,0:T(8,128)(2,1)S(1)}, u32[]{:S(2)}) copy-start(bf16[256,256]{1,0:T(8,128)(2,1)S(1)} %get-tuple-element.54.bc_ref) | copy-start | bytes 393220
  8.9 5.8 %copy-start.14 = (f32[40,256]{1,0:T(8,128)}, f32[40,256]{1,0:T(8,128)S(1)}, u32[]{:S(2)}) copy-start(f32[40,256]{1,0:T(8,128)S(1)} %get-tuple-element.55.log_ref) | copy-start | bytes 122884
  8.9 5.8 %copy-start.16 = (f32[40,256]{1,0:T(8,128)}, f32[40,256]{1,0:T(8,128)S(1)}, u32[]{:S(2)}) copy-start(f32[40,256]{1,0:T(8,128)S(1)} %get-tuple-element.60.dt_ref) | copy-start | bytes 122884
  8.9 3.4 %collective-permute-start = (f32[128,2688]{1,0:T(8,128)}, f32[128,2688]{1,0:T(8,128)S(1)}, u32[]{:S(2)}, u32[]{:S(2)}) collective-permute-start(f32[128,2688]{1,0:T(8,128)} %get-tuple-element.50), channel_id=1, source_target_pairs={{0,8},{8,0},{16,24},{24,16},{32,40},{40,32},{48,56},{56,48},{64,72... | collective-permute-start | bytes 4128776 | tf_op jit(solution)/shard_map/ppermute | solution.py:432
  12.3 2.4 %copy-start = (f32[128,2688]{1,0:T(8,128)}, f32[128,2688]{1,0:T(8,128)S(1)}, u32[]{:S(2)}) copy-start(f32[128,2688]{1,0:T(8,128)S(1)} %collective-permute-done.got_ref) | copy-start | bytes 4128772
  12.3 1.8 %copy-start.4 = (f32[128,2688]{1,0:T(8,128)S(1)}, f32[128,2688]{1,0:T(8,128)}, u32[]{:S(2)}) copy-start(f32[128,2688]{1,0:T(8,128)} %get-tuple-element.49.keep_ref) | copy-start | bytes 4128772
  14.7 1.1 copy-start.2
  15.8 27.3 %all-to-all-start = ((f32[16,8,2688]{2,1,0:T(8,128)}), f32[16,8,2688]{2,1,0:T(8,128)}, u32[]{:S(2)}, u32[]{:S(2)}) async-start(f32[16,8,2688]{2,1,0:T(8,128)} %bitcast.20), calls=%async_computation | async-start | bytes 2752512 | tf_op jit(solution)/shard_map/all_to_all | solution.py:437
  27.4 27.0 %collective-permute-start.2 = (f32[1280,256]{1,0:T(8,128)}, f32[1280,256]{1,0:T(8,128)}, u32[]{:S(2)}, u32[]{:S(2)}) collective-permute-start(f32[1280,256]{1,0:T(8,128)} %get-tuple-element.59), channel_id=1, source_target_pairs={{0,8},{8,0},{16,24},{24,16},{32,40},{40,32},{48,56},{56,48},{64,72... | collective-permute-start | bytes 3932168 | tf_op jit(solution)/shard_map/ppermute | solution.py:459
  27.4 27.0 %collective-permute-start.1 = (f32[64,2560]{1,0:T(8,128)}, f32[64,2560]{1,0:T(8,128)S(1)}, u32[]{:S(2)}, u32[]{:S(2)}) collective-permute-start(f32[64,2560]{1,0:T(8,128)} %get-tuple-element.58), channel_id=1, source_target_pairs={{0,8},{8,0},{16,24},{24,16},{32,40},{40,32},{48,56},{56,48},{64,72... | collective-permute-start | bytes 1966088 | tf_op jit(solution)/shard_map/ppermute | solution.py:460
  47.4 24.8 %all-to-all-start.1 = ((f32[16,8,2560]{2,1,0:T(8,128)}), f32[16,8,2560]{2,1,0:T(8,128)}, u32[]{:S(2)}, u32[]{:S(2)}) async-start(f32[16,8,2560]{2,1,0:T(8,128)} %copy-done.3), calls=%async_computation.1 | async-start | bytes 2621440 | tf_op jit(solution)/shard_map/all_to_all | solution.py:465
  72.2 3.8 %collective-permute-start.3 = (f32[128,2560]{1,0:T(8,128)}, f32[128,2560]{1,0:T(8,128)S(1)}, u32[]{:S(2)}, u32[]{:S(2)}) collective-permute-start(f32[128,2560]{1,0:T(8,128)} %bitcast.9.chip_ref), channel_id=1, source_target_pairs={{0,8},{8,0},{16,24},{24,16},{32,40},{40,32},{48,56},{56,48},{64,72... | collective-permute-start | bytes 3932168 | tf_op jit(solution)/shard_map/ppermute | solution.py:469
  72.2 1.3 %copy-start.1 = (f32[128,2688]{1,0:T(8,128)S(1)}, f32[128,2688]{1,0:T(8,128)}, u32[]{:S(2)}) copy-start(f32[128,2688]{1,0:T(8,128)} %copy-done) | copy-start | bytes 4128772
  73.5 2.5 %copy-start.7 = (f32[256,256]{1,0:T(8,128)S(1)}, f32[256,256]{1,0:T(8,128)}, u32[]{:S(2)}) copy-start(f32[256,256]{1,0:T(8,128)} %get-tuple-element.72.sgin_ref) | copy-start | bytes 786436
  76.0 1.9 %copy-start.9 = (f32[40,256]{1,0:T(8,128)S(1)}, f32[40,256]{1,0:T(8,128)}, u32[]{:S(2)}) copy-start(f32[40,256]{1,0:T(8,128)} %get-tuple-element.57.after_ref.cola_ref) | copy-start | bytes 122884
  76.0 1.8 %copy-start.11 = (bf16[256,256]{1,0:T(8,128)(2,1)S(1)}, bf16[256,256]{1,0:T(8,128)(2,1)}, u32[]{:S(2)}) copy-start(bf16[256,256]{1,0:T(8,128)(2,1)} %copy-done.10) | copy-start | bytes 393220
  76.0 1.8 %copy-start.15 = (f32[40,256]{1,0:T(8,128)S(1)}, f32[40,256]{1,0:T(8,128)}, u32[]{:S(2)}) copy-start(f32[40,256]{1,0:T(8,128)} %copy-done.14) | copy-start | bytes 122884
  76.0 1.8 %copy-start.17 = (f32[40,256]{1,0:T(8,128)S(1)}, f32[40,256]{1,0:T(8,128)}, u32[]{:S(2)}) copy-start(f32[40,256]{1,0:T(8,128)} %copy-done.16) | copy-start | bytes 122884
  76.0 1.8 %copy-start.18 = (f32[40,256]{1,0:T(8,128)S(1)}, f32[40,256]{1,0:T(8,128)}, u32[]{:S(2)}) copy-start(f32[40,256]{1,0:T(8,128)} %get-tuple-element.79.sig_ref) | copy-start | bytes 122884
  76.0 1.8 %copy-start.19 = (f32[40,256]{1,0:T(8,128)S(1)}, f32[40,256]{1,0:T(8,128)}, u32[]{:S(2)}) copy-start(f32[40,256]{1,0:T(8,128)} %get-tuple-element.80.crossa_ref) | copy-start | bytes 122884
  76.1 1.8 %copy-start.20 = (f32[40,256]{1,0:T(8,128)S(1)}, f32[40,256]{1,0:T(8,128)}, u32[]{:S(2)}) copy-start(f32[40,256]{1,0:T(8,128)} %get-tuple-element.81.crossb_ref) | copy-start | bytes 122884
  76.1 1.8 %copy-start.21 = (f32[40,256]{1,0:T(8,128)S(1)}, f32[40,256]{1,0:T(8,128)}, u32[]{:S(2)}) copy-start(f32[40,256]{1,0:T(8,128)} %get-tuple-element.82.colb_ref) | copy-start | bytes 122884
  76.1 1.8 %copy-start.22 = (f32[8,128]{1,0:T(8,128)S(1)}, f32[8,128]{1,0:T(8,128)}, u32[]{:S(2)}) copy-start(f32[8,128]{1,0:T(8,128)} %get-tuple-element.83.skip_ref) | copy-start | bytes 12292
  76.1 1.8 %copy-start.24 = (f32[40]{0:T(128)S(1)}, f32[40]{0:T(128)}, u32[]{:S(2)}) copy-start(f32[40]{0:T(128)} %param.14) | copy-start | bytes 484
  77.2 3.2 %copy-start.6 = (bf16[128,2560]{1,0:T(8,128)(2,1)}, bf16[128,2560]{1,0:T(8,128)(2,1)S(1)}, u32[]{:S(2)}) copy-start(bf16[128,2560]{1,0:T(8,128)(2,1)S(1)} %get-tuple-element.85.e_ref) | copy-start | bytes 1966084
  77.2 3.2 %copy-start.12 = (bf16[256,256]{1,0:T(8,128)(2,1)}, bf16[256,256]{1,0:T(8,128)(2,1)S(1)}, u32[]{:S(2)}) copy-start(bf16[256,256]{1,0:T(8,128)(2,1)S(1)} %get-tuple-element.89.sg_ref) | copy-start | bytes 393220
  77.2 4.3 %collective-permute-start.4 = (f32[256,256]{1,0:T(8,128)S(1)}, f32[256,256]{1,0:T(8,128)S(1)}, u32[]{:S(2)}, u32[]{:S(2)}) collective-permute-start(f32[256,256]{1,0:T(8,128)S(1)} %get-tuple-element.75), channel_id=1, source_target_pairs={{0,8},{8,0},{16,24},{24,16},{32,40},{40,32},{48,56},{56,48},{64,72... | collective-permute-start | bytes 786440 | tf_op jit(solution)/shard_map/ppermute | solution.py:484
  77.9 2.5 %copy-start.5 = (bf16[1280,256]{1,0:T(8,128)(2,1)S(1)}, bf16[1280,256]{1,0:T(8,128)(2,1)}, u32[]{:S(2)}) copy-start(bf16[1280,256]{1,0:T(8,128)(2,1)} %get-tuple-element.52.keep_ref) | copy-start | bytes 1966084
  80.4 1.2 collective-permute-start.5
  108.5 4.6 %collective-permute-start.6 = (f32[88,256]{1,0:T(8,128)S(1)}, f32[88,256]{1,0:T(8,128)S(1)}, u32[]{:S(2)}, u32[]{:S(2)}) collective-permute-start(f32[88,256]{1,0:T(8,128)S(1)} %reduce_sum.9), channel_id=1, source_target_pairs={{0,1},{1,0},{2,3},{3,2},{4,5},{5,4},{6,7},{7,6},{8,9},{9,8},{10,11... | collective-permute-start | bytes 270344 | tf_op jit(solution)/shard_map/ppermute | solution.py:511
  113.1 8.5 %collective-permute-start.7 = (f32[88,256]{1,0:T(8,128)S(1)}, f32[88,256]{1,0:T(8,128)S(1)}, u32[]{:S(2)}, u32[]{:S(2)}) collective-permute-start(f32[88,256]{1,0:T(8,128)S(1)} %add.9), channel_id=1, source_target_pairs={{0,2},{1,3},{2,0},{3,1},{4,6},{5,7},{6,4},{7,5},{8,10},{9,11},{10,... | collective-permute-start | bytes 270344 | tf_op jit(solution)/shard_map/ppermute | solution.py:511
  121.6 9.5 %collective-permute-start.8 = (f32[88,256]{1,0:T(8,128)S(1)}, f32[88,256]{1,0:T(8,128)S(1)}, u32[]{:S(2)}, u32[]{:S(2)}) collective-permute-start(f32[88,256]{1,0:T(8,128)S(1)} %add.10), channel_id=1, source_target_pairs={{0,4},{1,5},{2,6},{3,7},{4,0},{5,1},{6,2},{7,3},{8,12},{9,13},{10,... | collective-permute-start | bytes 270344 | tf_op jit(solution)/shard_map/ppermute | solution.py:511
  (5 other events, 3.9 us)

commit v3 on v2

--- a/solution.py
+++ b/solution.py
@@ -45,9 +45,9 @@
     return lax.dot_general(a, b, (((1,), (0,)), ((), ())), preferred_element_type=f32)
 
 
-def head_rows(count):
-    lane_head = iota((count, W), 1) >> 6
-    row = iota((count, W), 0)
+def head_rows(count, first=0, width=W):
+    lane_head = (iota((count, width), 1) + first) >> 6
+    row = iota((count, width), 0)
     hit = (lane_head == row) | (lane_head == row - H) | (lane_head == row - 2 * H)
     return jnp.where(hit, 1.0, 0.0).astype(bf16)
 
@@ -59,7 +59,7 @@
 
 def widen_row(row, spread):
     parts = jnp.concatenate(split3(row) + (jnp.zeros((8, 128), f32),), axis=0).astype(bf16)
-    lanes = iota((N, W), 0) < H
+    lanes = iota(spread.shape, 0) < H
     once = jnp.where(lanes, spread.astype(f32), 0.0).astype(bf16)
     out = dot10(parts, once)
     return out[0:8] + out[8:16] + out[16:24]
@@ -151,7 +151,7 @@
     out_ref[:, W:] = keep_ref[:, W:] * got_ref[:, W:]
 
 
-def scan_kernel(back_ref, in_ref, after_ref, out_ref, wide):
+def scan_kernel(back_ref, in_ref, out_ref, wide):
     spread = head_rows(N)
     for c in range(CHIPS):
         wide[c] = widen_row(in_ref[c, :, W:], spread)
@@ -322,7 +322,7 @@
 
 
 def logit_kernel(
-    s_ref, e_ref, meet_ref, xw_ref, ge_ref, bc_ref, log_ref, dt_ref, sig_ref, rate_ref,
+    s_ref, e_ref, meet_ref, x_ref, g_ref, bc_ref, log_ref, dt_ref, sig_ref, rate_ref,
     crossa_ref, crossb_ref, cola_ref, colb_ref, skip_ref,
     logit_ref, param_ref,
 ):
@@ -334,9 +334,14 @@
     last = log_decay[:, T - 1 : T]
     pick = spread[0:48]
     eb = dot10(b, e_ref[...])
-    v = dot11(pick, (xw_ref[...].astype(f32) * eb).astype(bf16))[0:H]
+
+    def head_sums(v):
+        hi = v.astype(bf16)
+        return dot11(pick, hi)[0:H]
+
+    v = jnp.exp(last - log_decay) * dt * head_sums(x_ref[...].astype(f32) * eb)
     from_start = dot10(c, s_ref[...])
-    carry = dot11(pick, (ge_ref[...].astype(f32) * from_start).astype(bf16))[0:H]
+    carry = jnp.exp(log_decay) * head_sums(g_ref[...].astype(f32) * from_start)
     meet = dot11(pick, jnp.concatenate(split3(meet_ref[...]), axis=0).astype(bf16))[0:H]
     through = jnp.sum(meet, axis=1, keepdims=True) * jnp.exp(last)
     row = iota((T, T), 0)
@@ -363,9 +368,9 @@
 
 
 def scan_grad_kernel(
-    e_ref, g_ref, bc_ref, log_ref, dt_ref, direct_ref, dua_ref, dub_ref, scan_ref
+    first, e_ref, g_ref, bc_ref, log_ref, dt_ref, direct_ref, du_ref, *rest
 ):
-    spread = head_rows(N)
+    spread = head_rows(N, first, W // 2)
     log_decay = log_ref[...]
     eb = dot10(bc_ref[:, :N], e_ref[...])
     to_end = widen(jnp.exp(log_decay[:, T - 1 : T] - log_decay) * dt_ref[...], spread)
@@ -373,12 +378,7 @@
         jnp.concatenate([direct_ref[...], jnp.zeros((1, 128 - H), f32)], axis=1), (8, 128)
     )
     direct = widen_row(direct_row, spread)[0:1]
-    half = W // 2
-    for at, ref in ((0, dua_ref), (half, dub_ref)):
-        to = slice(at, at + half)
-        scan_ref[:, to] = (
-            ref[...] + to_end[:, to] * eb[:, to] + direct[:, to] * g_ref[:, to].astype(f32)
-        ).astype(bf16)
+    rest[-1][...] = (du_ref[...] + to_end * eb + direct * g_ref[...].astype(f32)).astype(bf16)
 
 
 def mixer_kernel(sg_ref, proj_ref, mixer_ref):
@@ -427,7 +427,7 @@
             pltpu.VMEM((T, W), bf16), pltpu.VMEM((W, 2 * N), bf16), pltpu.VMEM((2 * N, W), f32),
             pltpu.SemaphoreType.DMA((5,)),
         ],
-        n_in=2, far=5, flops=int(1e9), moved=int(1e7), mib=50,
+        n_in=2, far=5, flops=int(1e9), moved=int(1e7), mib=54,
     )(core, bias_row, rate_row, lg, tok, x, g, proj)
     got = lax.ppermute(send, "seq", swap)
     (chips,) = call(
@@ -458,10 +458,11 @@
     )(core, tok_b, x, g, lg, bias_row)
     tokt_got = lax.ppermute(tokt_send, "seq", swap)
     more = lax.ppermute(more, "seq", swap)
+    owned, col_a = lax.optimization_barrier((owned, col_a))
     (starts,) = call(
         scan_kernel, [((CHIPS, 8, W), f32)], [pltpu.VMEM((CHIPS, 8, W), f32)],
-        n_in=2, flops=int(1e7), moved=int(3e6), mib=6,
-    )(back, owned, col_a)
+        n_in=1, flops=int(1e7), moved=int(3e6), mib=6,
+    )(back, owned)
     returned = exchange(starts).reshape(N, W)
     _, more, tokt_got, dt_b = lax.optimization_barrier((starts, more, tokt_got, dt))
     du_b, sg_b, cross_b, col_b = within(H // 4, dt_b, sg_a)
@@ -486,7 +487,7 @@
         logit_kernel, [((H, T), f32), ((8, 128), f32)], smem=0, n_in=15,
         flops=int(4e8), moved=int(4e6), mib=10,
     )(
-        s_all, e_all, meet, xw, ge, bc, log_decay, dt, sig, rate_row,
+        s_all, e_all, meet, x, g, bc, log_decay, dt, sig, rate_row,
         cross_a, cross_b, col_a, col_b, skip,
     )
     params_got = lax.ppermute(params, "seq", swap)
@@ -500,9 +501,34 @@
     )(own_weights, tokt_got, sg_got, params, params_got)
     parts = exchange(weights)
     parts, e_late, sg_late = lax.optimization_barrier((parts, e_all, sg))
-    (scan_grad,) = call(
-        scan_grad_kernel, [((T, W), bf16)], smem=0, n_in=8, flops=int(2e9), moved=int(1e7), mib=56,
-    )(e_late, g, bc, log_decay, dt, direct_row, du_a, du_b)
+    scan_grad = ()
+    for part, du in ((0, du_a), (1, du_b)):
+
+        def whole(shape):
+            return pl.BlockSpec(shape, lambda i: (0, 0))
+
+        def half_of(rows, part=part):
+            return pl.BlockSpec((rows, W // 2), lambda i: (0, part))
+
+        scan_grad = (
+            pl.pallas_call(
+                partial(scan_grad_kernel, part * (W // 2)),
+                grid=(1,),
+                out_shape=jax.ShapeDtypeStruct((T, W), bf16),
+                in_specs=[
+                    half_of(N), half_of(T), whole((T, 2 * N)), whole((H, T)), whole((H, T)),
+                    whole((1, H)), whole((T, W // 2)),
+                ]
+                + [pl.BlockSpec(memory_space=pl.ANY)] * part,
+                out_specs=half_of(T),
+                input_output_aliases={7: 0} if part else {},
+                compiler_params=pltpu.CompilerParams(vmem_limit_bytes=56 * 1024 * 1024),
+                cost_estimate=pl.CostEstimate(
+                    flops=int(1e9), bytes_accessed=int(5e6), transcendentals=0
+                ),
+            )(e_late, g, bc, log_decay, dt, direct_row, du, *scan_grad),
+        )
+    (scan_grad,) = scan_grad
     (mixer_grad,) = call(
         mixer_kernel, [((T, W), bf16)], smem=0, n_in=2, flops=int(1e9), moved=int(3e6), mib=56,
     )(sg_late, proj)

time: 133 us -> 129 us (0.970)
  waiting for transfers between devices: 21.2 us -> 17.3 us
  local copies, waits for them, and re-layouts: 10.2 us -> 6.86 us
    ppermute x3, waiting for transfers between devices: 3.61 us -> 0.27 us  [on_device(): total = total + lax.ppermute(total, 'dp', [(i, i ^ k) for i in range(8)])]
    unnamed x52 -> x44, local copies, waits for them, and re-layouts: 8.27 us -> 4.98 us
    pallas_call x1 -> x2, Pallas kernels: 5.15 us -> 6.88 us  [on_device(): pl.pallas_call(partial(scan_grad_kernel, part * (W // 2)), grid=(1,), out...]
    pallas_call x1, Pallas kernels: 2.47 us -> 1.13 us  [on_device(): call(scan_kernel, [((CHIPS, 8, W), f32)], [pltpu.VMEM((CHIPS, 8, W), f32)...]
  transfers between devices with their start and end apart: 11 -> 11, of which waited for: 6 -> 5; matrix products, arithmetic and copies ran while one was open for 1% -> 1% of each run, Pallas kernels for 29% -> 31%
where the time goes in v3:
time: 129 us; the launch traced here: 128 us
  Pallas kernels  49.5 us (38%)
  starting transfers between devices  27.8 us (22%)
  blocking collectives  25.4 us (20%)
  waiting for transfers between devices  17.3 us (13%)
  local copies, waits for them, and re-layouts  6.86 us (5%)
    all_to_all x1, blocking collectives, on_device(): parts = exchange(weights)  25.4 us
    pallas_call x2, Pallas kernels, within(): call(partial(within_kernel, first), [((T, W // 2), f32), ((T, 2 * N), f32...  18.9 us
    ppermute x3, starting transfers between devices, on_device(): total = total + lax.ppermute(total, 'dp', [(i, i ^ k) for i in range(8)])  11.8 us
    all_to_all x1, waiting for transfers between devices, on_device(): returned = exchange(starts).reshape(N, W)  8.21 us
    all_to_all x1, starting transfers between devices, on_device(): owned = exchange(chips.reshape(CHIPS, 8, W + TAIL))  7.48 us
    all_to_all x1, starting transfers between devices, on_device(): returned = exchange(starts).reshape(N, W)  6.95 us
    pallas_call x1, Pallas kernels, on_device(): call(summary_kernel, [((T, 2 * N), bf16), ((T, W), bf16), ((T, W), bf16),...  6.93 us
    pallas_call x2, Pallas kernels, on_device(): pl.pallas_call(partial(scan_grad_kernel, part * (W // 2)), grid=(1,), out...  6.88 us
  transfers between devices with their start and end apart: 11, of which 5 were waited for; matrix products, arithmetic and copies ran while one was open for 1% of the time, Pallas kernels for 31%

profile of v3, /device:TPU:2, one launch (start us, length us, event | category | flops | bytes accessed | tf_op | source)
XLA Modules:
  0.0 127.9 jit_solution(3707848836897221265)
XLA Ops:
  0.6 6.9 %shard_map.135 = (bf16[256,256]{1,0:T(8,128)(2,1)}, bf16[256,2560]{1,0:T(8,128)(2,1)}, bf16[256,2560]{1,0:T(8,128)(2,1)}, f32[128,2688]{1,0:T(8,128)}, f32[128,2...) custom-call(s32[1]{0:T(128)} %bitcast.core_ref, f32[1,40]{1,0:T(1,128)} %bitcast.42, ...), custom_call_target="tpu_custom_call" | custom-call | flops 1000000000 | bytes 10000000 | tf_op jit(solution)/shard_map/pallas_call | solution.py:418
  7.7 3.3 %collective-permute-done.got_ref = f32[128,2688]{1,0:T(8,128)S(1)} collective-permute-done((f32[128,2688]{1,0:T(8,128)}, f32[128,2688]{1,0:T(8,128)S(1)}, u32[]{:S(2)}, u32[]{:S(2)}) %collective-permute-start) | collective-permute-done | bytes 1376288 | tf_op jit(solution)/shard_map/ppermute | solution.py:432
  11.0 1.3 %copy-done.8 = f32[128,2688]{1,0:T(8,128)S(1)} copy-done((f32[128,2688]{1,0:T(8,128)S(1)}, f32[128,2688]{1,0:T(8,128)}, u32[]{:S(2)}) %copy-start.8) | copy-done | bytes 1376280
  12.3 0.5 shard_map.136
  12.8 1.1 copy-done.2
  13.9 7.5 %all-to-all-start = ((f32[16,8,2688]{2,1,0:T(8,128)}), f32[16,8,2688]{2,1,0:T(8,128)S(1)}, u32[]{:S(2)}, u32[]{:S(2)}) async-start(f32[16,8,2688]{2,1,0:T(8,128)} %bitcast.27), calls=%async_computation | async-start | bytes 2752512 | tf_op jit(solution)/shard_map/all_to_all | solution.py:437
  21.4 4.1 %shard_map.137 = (bf16[1280,256]{1,0:T(8,128)(2,1)}, f32[1280,256]{1,0:T(8,128)}, f32[40,256]{1,0:T(8,128)}, f32[8,128]{1,0:T(8,128)}) custom-call(s32[1]{0:T(128)} %bitcast.core_ref, bf16[256,2560]{1,0:T(8,128)(2,1)} %bitcast.37, bf16[256,2560]{1,0:T(8,128)(2,1)} %bitcast.29, bf16[256,2560]{1,0:T(8,128)(2,1)} %bitcast.21, f32[40,256]{1,0:T(8,128)} %bitcast.39, ...), custom_call_target="tpu_custom_call" | custom-call | flops 3000000000 | bytes 8000000 | tf_op jit(solution)/shard_map/pallas_call | solution.py:451
  25.5 0.5 collective-permute-start.1
  26.0 0.7 broadcast_in_dim.12.before_ref
  26.7 9.4 %shard_map.138 = (f32[256,1280]{1,0:T(8,128)}, f32[256,256]{1,0:T(8,128)}, f32[40,256]{1,0:T(8,128)}, f32[40,256]{1,0:T(8,128)}) custom-call(bf16[256,2560]{1,0:T(8,128)(2,1)} %bitcast.30, bf16[256,2560]{1,0:T(8,128)(2,1)} %bitcast.22, bf16[256,256]{1,0:T(8,128)(2,1)} %get-tuple-element.56.bc_ref, f32[40,256]{1,0:T(8,128)} %get-tuple-element.57.log_ref, ...), custom_call_target="tpu_custom_call" | custom-call | flops 8000000000 | bytes 5000000 | tf_op jit(solution)/shard_map/pallas_call | solution.py:440
  36.1 5.0 %all-to-all-done.in_ref = f32[16,8,2688]{2,1,0:T(8,128)S(1)} async-done(((f32[16,8,2688]{2,1,0:T(8,128)}), f32[16,8,2688]{2,1,0:T(8,128)S(1)}, u32[]{:S(2)}, u32[]{:S(2)}) %all-to-all-start) | async-done | bytes 1376288 | tf_op jit(solution)/shard_map/all_to_all | solution.py:437
  41.1 1.1 shard_map.139
  42.3 1.1 copy-done.6
  43.4 7.0 %all-to-all-start.1 = ((f32[16,8,2560]{2,1,0:T(8,128)}), f32[16,8,2560]{2,1,0:T(8,128)}, u32[]{:S(2)}, u32[]{:S(2)}) async-start(f32[16,8,2560]{2,1,0:T(8,128)} %copy-done.6), calls=%async_computation.1 | async-start | bytes 2621440 | tf_op jit(solution)/shard_map/all_to_all | solution.py:466
  50.4 9.5 %shard_map.140 = (f32[256,1280]{1,0:T(8,128)}, f32[256,256]{1,0:T(8,128)}, f32[40,256]{1,0:T(8,128)}, f32[40,256]{1,0:T(8,128)}) custom-call(bf16[256,2560]{1,0:T(8,128)(2,1)} %bitcast.31, bf16[256,2560]{1,0:T(8,128)(2,1)} %bitcast.23, bf16[256,256]{1,0:T(8,128)(2,1)} %get-tuple-element.56.bc_ref, f32[40,256]{1,0:T(8,128)} %get-tuple-element.57.log_ref, ...), custom_call_target="tpu_custom_call" | custom-call | flops 8000000000 | bytes 5000000 | tf_op jit(solution)/shard_map/pallas_call | solution.py:440
  59.9 8.2 %all-to-all-done.1 = f32[16,8,2560]{2,1,0:T(8,128)} async-done(((f32[16,8,2560]{2,1,0:T(8,128)}), f32[16,8,2560]{2,1,0:T(8,128)}, u32[]{:S(2)}, u32[]{:S(2)}) %all-to-all-start.1) | async-done | bytes 1310752 | tf_op jit(solution)/shard_map/all_to_all | solution.py:466
  68.1 1.3 %copy-done.4 = bf16[256,2560]{1,0:T(8,128)(2,1)S(1)} copy-done((bf16[256,2560]{1,0:T(8,128)(2,1)S(1)}, bf16[256,2560]{1,0:T(8,128)(2,1)}, u32[]{:S(2)}) %copy-start.4) | copy-done | bytes 1310744
  69.5 2.5 %shard_map.141 = (bf16[64,2560]{1,0:T(8,128)(2,1)S(1)}, bf16[64,2560]{1,0:T(8,128)(2,1)S(1)}, f32[8,2560]{1,0:T(8,128)S(1)}, f32[256,128]{1,0:T(8,128)S(1)}, f32[8,128]{1,0:T(8,128)S(1)}) custom-call(s32[1]{0:T(128)} %bitcast.core_ref, f32[128,2560]{1,0:T(8,128)} %bitcast.9.chip_ref, f32[128,2688]{1,0:T(8,128)S(1)} %collective-permute-done.got_ref, ...), custom_call_target="tpu_custom_call" | custom-call | flops 400000000 | bytes 6000000 | tf_op jit(solution)/shard_map/pallas_call | solution.py:471
  72.1 1.1 shard_map.142
  73.3 0.6 collective-permute-start.4
  74.0 2.4 %shard_map.144 = (f32[40,256]{1,0:T(8,128)}, f32[8,128]{1,0:T(8,128)S(1)}) custom-call(bf16[128,2560]{1,0:T(8,128)(2,1)S(1)} %get-tuple-element.79.s_ref, bf16[128,2560]{1,0:T(8,128)(2,1)S(1)} %get-tuple-element.89.e_ref, f32[8,2560]{1,0:T(8,128)S(1)} %get-tuple-element.81.meet_ref, bf16[256,2560]{1,0:T(8,128)(2,1)S(1)} %bitcast.32, ...), custom_call_target="tpu_custom_call" | custom-call | flops 400000000 | bytes 4000000 | tf_op jit(solution)/shard_map/pallas_call | solution.py:486
  77.1 0.5 collective-permute-done.5.paramgot_ref
  77.6 1.7 %shard_map.145 = f32[16,88,256]{2,1,0:T(8,128)S(1)} custom-call(f32[1280,256]{1,0:T(8,128)S(1)} %shard_map.143.own_ref, f32[1280,256]{1,0:T(8,128)} %collective-permute-done.2.got_ref, f32[256,256]{1,0:T(8,128)S(1)} %collective-permute-done.4.sggot_ref, f32[8,128]{1,0:T(8,128)S(1)} %get-tuple-element.88.param_ref, ...), custom_call_target="tpu_custom_call" | custom-call | flops 200000000 | bytes 4000000 | tf_op jit(solution)/shard_map/pallas_call | solution.py:498
  79.3 25.4 %all_to_all.15 = f32[16,88,256]{2,1,0:T(8,128)S(1)} all-to-all(f32[16,88,256]{2,1,0:T(8,128)S(1)} %shard_map.145), channel_id=1, replica_groups={{0,16,32,48,64,80,96,112,128,144,160,176,192,208,224,240},{8,24,40,56,7..., dimensions={0} | all-to-all | bytes 2883584 | tf_op jit(solution)/shard_map/all_to_all | solution.py:502
  104.7 2.0 %collective-permute-start.6 = (f32[88,256]{1,0:T(8,128)S(1)}, f32[88,256]{1,0:T(8,128)S(1)}, u32[]{:S(2)}, u32[]{:S(2)}) collective-permute-start(f32[88,256]{1,0:T(8,128)S(1)} %reduce_sum.9), channel_id=1, source_target_pairs={{0,1},{1,0},{2,3},{3,2},{4,5},{5,4},{6,7},{7,6},{8,9},{9,8},{10,11... | collective-permute-start | bytes 270344 | tf_op jit(solution)/shard_map/ppermute | solution.py:537
  106.8 3.0 %shard_map.148 = bf16[256,2560]{1,0:T(8,128)(2,1)} custom-call(bf16[256,256]{1,0:T(8,128)(2,1)} %copy-done.14, bf16[2560,256]{1,0:T(8,128)(2,1)} %proj_ref.1), custom_call_target="tpu_custom_call" | custom-call | flops 1000000000 | bytes 3000000 | tf_op jit(solution)/shard_map/pallas_call | solution.py:532
  109.8 3.3 %collective-permute-start.7 = (f32[88,256]{1,0:T(8,128)S(1)}, f32[88,256]{1,0:T(8,128)S(1)}, u32[]{:S(2)}, u32[]{:S(2)}) collective-permute-start(f32[88,256]{1,0:T(8,128)S(1)} %add.9), channel_id=1, source_target_pairs={{0,2},{1,3},{2,0},{3,1},{4,6},{5,7},{6,4},{7,5},{8,10},{9,11},{10,... | collective-permute-start | bytes 270344 | tf_op jit(solution)/shard_map/ppermute | solution.py:537
  113.1 3.4 %shard_map.146.rest_0_ = bf16[256,2560]{1,0:T(8,128)(2,1)} custom-call(bf16[128,2560]{1,0:T(8,128)(2,1)} %copy-done.1, bf16[256,2560]{1,0:T(8,128)(2,1)} %bitcast.24, bf16[256,256]{1,0:T(8,128)(2,1)} %get-tuple-element.56.bc_ref, f32[40,256]{1,0:T(8,128)} %get-tuple-element.57.log_ref, f32[40,256]{1,0:T(8,128)} %get-tuple-element.63.dt_ref, ...), custom_call_target="tpu_custom_call" | custom-call | flops 1000000000 | bytes 5000000 | tf_op jit(solution)/shard_map/pallas_call | solution.py:514
  116.8 6.5 %collective-permute-start.8 = (f32[88,256]{1,0:T(8,128)S(1)}, f32[88,256]{1,0:T(8,128)S(1)}, u32[]{:S(2)}, u32[]{:S(2)}) collective-permute-start(f32[88,256]{1,0:T(8,128)S(1)} %add.10), channel_id=1, source_target_pairs={{0,4},{1,5},{2,6},{3,7},{4,0},{5,1},{6,2},{7,3},{8,12},{9,13},{10,... | collective-permute-start | bytes 270344 | tf_op jit(solution)/shard_map/ppermute | solution.py:537
  123.3 3.4 %shard_map.147 = bf16[256,2560]{1,0:T(8,128)(2,1)} custom-call(bf16[128,2560]{1,0:T(8,128)(2,1)} %copy-done.1, bf16[256,2560]{1,0:T(8,128)(2,1)} %bitcast.25, bf16[256,256]{1,0:T(8,128)(2,1)} %get-tuple-element.56.bc_ref, f32[40,256]{1,0:T(8,128)} %get-tuple-element.57.log_ref, f32[40,256]{1,0:T(8,128)} %get-tuple-element.63.dt_ref, ...), custom_call_target="tpu_custom_call", output_to_operand_aliasing={{}: (7, {})} | custom-call | flops 1000000000 | bytes 5000000 | tf_op jit(solution)/shard_map/pallas_call | solution.py:514
  126.8 0.5 slice_bitcast_fusion
  127.3 0.6 slice.16
  (56 shorter events, 1.2 us)
Async XLA Ops:
  7.6 3.4 %collective-permute-start = (f32[128,2688]{1,0:T(8,128)}, f32[128,2688]{1,0:T(8,128)S(1)}, u32[]{:S(2)}, u32[]{:S(2)}) collective-permute-start(f32[128,2688]{1,0:T(8,128)} %get-tuple-element.52), channel_id=1, source_target_pairs={{0,8},{8,0},{16,24},{24,16},{32,40},{40,32},{48,56},{56,48},{64,72... | collective-permute-start | bytes 4128776 | tf_op jit(solution)/shard_map/ppermute | solution.py:432
  11.0 1.3 %copy-start.8 = (f32[128,2688]{1,0:T(8,128)S(1)}, f32[128,2688]{1,0:T(8,128)}, u32[]{:S(2)}) copy-start(f32[128,2688]{1,0:T(8,128)} %get-tuple-element.51.keep_ref) | copy-start | bytes 4128772
  13.9 27.2 %all-to-all-start = ((f32[16,8,2688]{2,1,0:T(8,128)}), f32[16,8,2688]{2,1,0:T(8,128)S(1)}, u32[]{:S(2)}, u32[]{:S(2)}) async-start(f32[16,8,2688]{2,1,0:T(8,128)} %bitcast.27), calls=%async_computation | async-start | bytes 2752512 | tf_op jit(solution)/shard_map/all_to_all | solution.py:437
  25.5 24.9 %collective-permute-start.2 = (f32[1280,256]{1,0:T(8,128)}, f32[1280,256]{1,0:T(8,128)}, u32[]{:S(2)}, u32[]{:S(2)}) collective-permute-start(f32[1280,256]{1,0:T(8,128)} %get-tuple-element.62), channel_id=1, source_target_pairs={{0,8},{8,0},{16,24},{24,16},{32,40},{40,32},{48,56},{56,48},{64,72... | collective-permute-start | bytes 3932168 | tf_op jit(solution)/shard_map/ppermute | solution.py:459
  25.5 24.8 %collective-permute-start.1 = (f32[64,2560]{1,0:T(8,128)}, f32[64,2560]{1,0:T(8,128)S(1)}, u32[]{:S(2)}, u32[]{:S(2)}) collective-permute-start(f32[64,2560]{1,0:T(8,128)} %get-tuple-element.61), channel_id=1, source_target_pairs={{0,8},{8,0},{16,24},{24,16},{32,40},{40,32},{48,56},{56,48},{64,72... | collective-permute-start | bytes 1966088 | tf_op jit(solution)/shard_map/ppermute | solution.py:460
  42.2 1.2 copy-start.6
  43.4 24.7 %all-to-all-start.1 = ((f32[16,8,2560]{2,1,0:T(8,128)}), f32[16,8,2560]{2,1,0:T(8,128)}, u32[]{:S(2)}, u32[]{:S(2)}) async-start(f32[16,8,2560]{2,1,0:T(8,128)} %copy-done.6), calls=%async_computation.1 | async-start | bytes 2621440 | tf_op jit(solution)/shard_map/all_to_all | solution.py:466
  50.4 17.8 %copy-start.3 = (bf16[256,2560]{1,0:T(8,128)(2,1)S(1)}, bf16[256,2560]{1,0:T(8,128)(2,1)}, u32[]{:S(2)}) copy-start(bf16[256,2560]{1,0:T(8,128)(2,1)} %get-tuple-element.68.xw_ref) | copy-start | bytes 3932164
  68.1 3.9 %collective-permute-start.3 = (f32[128,2560]{1,0:T(8,128)}, f32[128,2560]{1,0:T(8,128)S(1)}, u32[]{:S(2)}, u32[]{:S(2)}) collective-permute-start(f32[128,2560]{1,0:T(8,128)} %bitcast.9.chip_ref), channel_id=1, source_target_pairs={{0,8},{8,0},{16,24},{24,16},{32,40},{40,32},{48,56},{56,48},{64,72... | collective-permute-start | bytes 3932168 | tf_op jit(solution)/shard_map/ppermute | solution.py:470
  68.1 1.3 %copy-start.4 = (bf16[256,2560]{1,0:T(8,128)(2,1)S(1)}, bf16[256,2560]{1,0:T(8,128)(2,1)}, u32[]{:S(2)}) copy-start(bf16[256,2560]{1,0:T(8,128)(2,1)} %get-tuple-element.69.ge_ref) | copy-start | bytes 3932164
  69.5 2.5 %copy-start.5 = (bf16[256,2560]{1,0:T(8,128)(2,1)S(1)}, bf16[256,2560]{1,0:T(8,128)(2,1)}, u32[]{:S(2)}) copy-start(bf16[256,2560]{1,0:T(8,128)(2,1)} %get-tuple-element.69.ge_ref) | copy-start | bytes 3932164
  69.5 2.5 %copy-start.13 = (f32[256,256]{1,0:T(8,128)S(1)}, f32[256,256]{1,0:T(8,128)}, u32[]{:S(2)}) copy-start(f32[256,256]{1,0:T(8,128)} %get-tuple-element.75.sgin_ref) | copy-start | bytes 786436
  72.0 1.9 %copy-start = (bf16[1,256,2560]{2,1,0:T(8,128)(2,1)S(1)}, bf16[1,256,2560]{2,1,0:T(8,128)(2,1)}, u32[]{:S(2)}) copy-start(bf16[1,256,2560]{2,1,0:T(8,128)(2,1)} %param.11) | copy-start | bytes 3932164
  72.0 1.9 %copy-start.7 = (bf16[1,256,2560]{2,1,0:T(8,128)(2,1)S(1)}, bf16[1,256,2560]{2,1,0:T(8,128)(2,1)}, u32[]{:S(2)}) copy-start(bf16[1,256,2560]{2,1,0:T(8,128)(2,1)} %param.9) | copy-start | bytes 3932164
  72.0 1.9 %copy-start.9 = (bf16[256,256]{1,0:T(8,128)(2,1)S(1)}, bf16[256,256]{1,0:T(8,128)(2,1)}, u32[]{:S(2)}) copy-start(bf16[256,256]{1,0:T(8,128)(2,1)} %get-tuple-element.56.bc_ref) | copy-start | bytes 393220
  72.0 1.9 %copy-start.11 = (f32[40,256]{1,0:T(8,128)S(1)}, f32[40,256]{1,0:T(8,128)}, u32[]{:S(2)}) copy-start(f32[40,256]{1,0:T(8,128)} %get-tuple-element.57.log_ref) | copy-start | bytes 122884
  72.1 1.9 %copy-start.12 = (f32[40,256]{1,0:T(8,128)S(1)}, f32[40,256]{1,0:T(8,128)}, u32[]{:S(2)}) copy-start(f32[40,256]{1,0:T(8,128)} %get-tuple-element.63.dt_ref) | copy-start | bytes 122884
  72.1 1.9 %copy-start.15 = (f32[40,256]{1,0:T(8,128)S(1)}, f32[40,256]{1,0:T(8,128)}, u32[]{:S(2)}) copy-start(f32[40,256]{1,0:T(8,128)} %get-tuple-element.82.sig_ref) | copy-start | bytes 122884
  72.1 1.9 %copy-start.16 = (f32[40,256]{1,0:T(8,128)S(1)}, f32[40,256]{1,0:T(8,128)}, u32[]{:S(2)}) copy-start(f32[40,256]{1,0:T(8,128)} %get-tuple-element.83.crossa_ref) | copy-start | bytes 122884
  72.1 1.9 %copy-start.17 = (f32[40,256]{1,0:T(8,128)S(1)}, f32[40,256]{1,0:T(8,128)}, u32[]{:S(2)}) copy-start(f32[40,256]{1,0:T(8,128)} %get-tuple-element.85.cola_ref) | copy-start | bytes 122884
  72.1 1.9 %copy-start.18 = (f32[40,256]{1,0:T(8,128)S(1)}, f32[40,256]{1,0:T(8,128)}, u32[]{:S(2)}) copy-start(f32[40,256]{1,0:T(8,128)} %get-tuple-element.84.crossb_ref) | copy-start | bytes 122884
  72.1 1.9 %copy-start.19 = (f32[40,256]{1,0:T(8,128)S(1)}, f32[40,256]{1,0:T(8,128)}, u32[]{:S(2)}) copy-start(f32[40,256]{1,0:T(8,128)} %get-tuple-element.86.colb_ref) | copy-start | bytes 122884
  72.1 1.9 %copy-start.20 = (f32[8,128]{1,0:T(8,128)S(1)}, f32[8,128]{1,0:T(8,128)}, u32[]{:S(2)}) copy-start(f32[8,128]{1,0:T(8,128)} %get-tuple-element.87.skip_ref) | copy-start | bytes 12292
  72.1 1.9 %copy-start.21 = (f32[40]{0:T(128)S(1)}, f32[40]{0:T(128)}, u32[]{:S(2)}) copy-start(f32[40]{0:T(128)} %param.14) | copy-start | bytes 484
  73.3 3.2 %copy-start.1 = (bf16[128,2560]{1,0:T(8,128)(2,1)}, bf16[128,2560]{1,0:T(8,128)(2,1)S(1)}, u32[]{:S(2)}) copy-start(bf16[128,2560]{1,0:T(8,128)(2,1)S(1)} %get-tuple-element.89.e_ref) | copy-start | bytes 1966084
  73.3 3.5 %copy-start.14 = (bf16[256,256]{1,0:T(8,128)(2,1)}, bf16[256,256]{1,0:T(8,128)(2,1)S(1)}, u32[]{:S(2)}) copy-start(bf16[256,256]{1,0:T(8,128)(2,1)S(1)} %get-tuple-element.93.sg_ref) | copy-start | bytes 393220
  73.3 4.3 %collective-permute-start.4 = (f32[256,256]{1,0:T(8,128)S(1)}, f32[256,256]{1,0:T(8,128)S(1)}, u32[]{:S(2)}, u32[]{:S(2)}) collective-permute-start(f32[256,256]{1,0:T(8,128)S(1)} %get-tuple-element.78), channel_id=1, source_target_pairs={{0,8},{8,0},{16,24},{24,16},{32,40},{40,32},{48,56},{56,48},{64,72... | collective-permute-start | bytes 786440 | tf_op jit(solution)/shard_map/ppermute | solution.py:485
  74.0 2.8 %copy-start.10 = (bf16[1280,256]{1,0:T(8,128)(2,1)S(1)}, bf16[1280,256]{1,0:T(8,128)(2,1)}, u32[]{:S(2)}) copy-start(bf16[1280,256]{1,0:T(8,128)(2,1)} %get-tuple-element.54.keep_ref) | copy-start | bytes 1966084
  76.4 1.2 collective-permute-start.5
  104.7 5.0 %collective-permute-start.6 = (f32[88,256]{1,0:T(8,128)S(1)}, f32[88,256]{1,0:T(8,128)S(1)}, u32[]{:S(2)}, u32[]{:S(2)}) collective-permute-start(f32[88,256]{1,0:T(8,128)S(1)} %reduce_sum.9), channel_id=1, source_target_pairs={{0,1},{1,0},{2,3},{3,2},{4,5},{5,4},{6,7},{7,6},{8,9},{9,8},{10,11... | collective-permute-start | bytes 270344 | tf_op jit(solution)/shard_map/ppermute | solution.py:537
  109.8 7.0 %collective-permute-start.7 = (f32[88,256]{1,0:T(8,128)S(1)}, f32[88,256]{1,0:T(8,128)S(1)}, u32[]{:S(2)}, u32[]{:S(2)}) collective-permute-start(f32[88,256]{1,0:T(8,128)S(1)} %add.9), channel_id=1, source_target_pairs={{0,2},{1,3},{2,0},{3,1},{4,6},{5,7},{6,4},{7,5},{8,10},{9,11},{10,... | collective-permute-start | bytes 270344 | tf_op jit(solution)/shard_map/ppermute | solution.py:537
  116.8 10.0 %collective-permute-start.8 = (f32[88,256]{1,0:T(8,128)S(1)}, f32[88,256]{1,0:T(8,128)S(1)}, u32[]{:S(2)}, u32[]{:S(2)}) collective-permute-start(f32[88,256]{1,0:T(8,128)S(1)} %add.10), channel_id=1, source_target_pairs={{0,4},{1,5},{2,6},{3,7},{4,0},{5,1},{6,2},{7,3},{8,12},{9,13},{10,... | collective-permute-start | bytes 270344 | tf_op jit(solution)/shard_map/ppermute | solution.py:537
  (1 other events, 1.1 us)

commit v4 on v3

--- a/solution.py
+++ b/solution.py
@@ -108,15 +108,17 @@
     last = log_decay[:, T - 1 : T]
     log_ref[...] = log_decay
     dt_ref[...] = dt
+    to_end = widen(jnp.exp(last - log_decay) * dt, spread)
+    from_start = widen(jnp.exp(log_decay), spread)
     copies[1].wait()
     copies[2].wait()
     bc = dot10(tok_ref[...], proj_ref[...]).astype(bf16)
     bc_ref[...] = bc
     copies[3].wait()
     copies[4].wait()
-    xw = (x_ref[...].astype(f32) * widen(jnp.exp(last - log_decay) * dt, spread)).astype(bf16)
+    xw = (x_ref[...].astype(f32) * to_end).astype(bf16)
     xw_ref[...] = xw
-    ge = (g_ref[...].astype(f32) * widen(jnp.exp(log_decay), spread)).astype(bf16)
+    ge = (g_ref[...].astype(f32) * from_start).astype(bf16)
     ge_ref[...] = ge
     both[0:N, :] = dot00(bc[:, :N], xw)
     both[N : 2 * N, :] = dot00(bc[:, N:], ge)

time: 129 us -> 128 us (level)
  no operation moved by 1% of the time
where the time goes in v4:
time: 128 us
  Pallas kernels  49.2 us (38%)
  starting transfers between devices  27.8 us (22%)
  blocking collectives  25.4 us (20%)
  waiting for transfers between devices  17.3 us (14%)
  local copies, waits for them, and re-layouts  6.86 us (5%)
    all_to_all x1, blocking collectives, on_device(): parts = exchange(weights)  25.4 us
    pallas_call x2, Pallas kernels, within(): call(partial(within_kernel, first), [((T, W // 2), f32), ((T, 2 * N), f32...  18.9 us
    ppermute x3, starting transfers between devices, on_device(): total = total + lax.ppermute(total, 'dp', [(i, i ^ k) for i in range(8)])  11.8 us
    all_to_all x1, waiting for transfers between devices, on_device(): returned = exchange(starts).reshape(N, W)  8.24 us
    all_to_all x1, starting transfers between devices, on_device(): owned = exchange(chips.reshape(CHIPS, 8, W + TAIL))  7.48 us
    all_to_all x1, starting transfers between devices, on_device(): returned = exchange(starts).reshape(N, W)  6.97 us
    pallas_call x2, Pallas kernels, on_device(): pl.pallas_call(partial(scan_grad_kernel, part * (W // 2)), grid=(1,), out...  6.9 us
    pallas_call x1, Pallas kernels, on_device(): call(summary_kernel, [((T, 2 * N), bf16), ((T, W), bf16), ((T, W), bf16),...  6.59 us
  transfers between devices with their start and end apart: 11, of which 5 were waited for; matrix products, arithmetic and copies ran while one was open for 1% of the time, Pallas kernels for 31%

profile of v4, /device:TPU:2, one launch (start us, length us, event | category | flops | bytes accessed | tf_op | source)
XLA Modules:
  0.0 127.6 jit_solution(14729652868694656444)
XLA Ops:
  0.6 6.6 %shard_map.135 = (bf16[256,256]{1,0:T(8,128)(2,1)}, bf16[256,2560]{1,0:T(8,128)(2,1)}, bf16[256,2560]{1,0:T(8,128)(2,1)}, f32[128,2688]{1,0:T(8,128)}, f32[128,2...) custom-call(s32[1]{0:T(128)} %bitcast.core_ref, f32[1,40]{1,0:T(1,128)} %bitcast.42, ...), custom_call_target="tpu_custom_call" | custom-call | flops 1000000000 | bytes 10000000 | tf_op jit(solution)/shard_map/pallas_call | solution.py:420
  7.3 3.3 %collective-permute-done.got_ref = f32[128,2688]{1,0:T(8,128)S(1)} collective-permute-done((f32[128,2688]{1,0:T(8,128)}, f32[128,2688]{1,0:T(8,128)S(1)}, u32[]{:S(2)}, u32[]{:S(2)}) %collective-permute-start) | collective-permute-done | bytes 1376288 | tf_op jit(solution)/shard_map/ppermute | solution.py:434
  10.7 1.3 %copy-done.8 = f32[128,2688]{1,0:T(8,128)S(1)} copy-done((f32[128,2688]{1,0:T(8,128)S(1)}, f32[128,2688]{1,0:T(8,128)}, u32[]{:S(2)}) %copy-start.8) | copy-done | bytes 1376280
  12.0 0.5 shard_map.136
  12.5 1.1 copy-done.2
  13.6 7.5 %all-to-all-start = ((f32[16,8,2688]{2,1,0:T(8,128)}), f32[16,8,2688]{2,1,0:T(8,128)S(1)}, u32[]{:S(2)}, u32[]{:S(2)}) async-start(f32[16,8,2688]{2,1,0:T(8,128)} %bitcast.27), calls=%async_computation | async-start | bytes 2752512 | tf_op jit(solution)/shard_map/all_to_all | solution.py:439
  21.1 4.1 %shard_map.137 = (bf16[1280,256]{1,0:T(8,128)(2,1)}, f32[1280,256]{1,0:T(8,128)}, f32[40,256]{1,0:T(8,128)}, f32[8,128]{1,0:T(8,128)}) custom-call(s32[1]{0:T(128)} %bitcast.core_ref, bf16[256,2560]{1,0:T(8,128)(2,1)} %bitcast.37, bf16[256,2560]{1,0:T(8,128)(2,1)} %bitcast.29, bf16[256,2560]{1,0:T(8,128)(2,1)} %bitcast.21, f32[40,256]{1,0:T(8,128)} %bitcast.39, ...), custom_call_target="tpu_custom_call" | custom-call | flops 3000000000 | bytes 8000000 | tf_op jit(solution)/shard_map/pallas_call | solution.py:453
  25.2 0.5 collective-permute-start.1
  25.7 0.7 broadcast_in_dim.12.before_ref
  26.4 9.4 %shard_map.138 = (f32[256,1280]{1,0:T(8,128)}, f32[256,256]{1,0:T(8,128)}, f32[40,256]{1,0:T(8,128)}, f32[40,256]{1,0:T(8,128)}) custom-call(bf16[256,2560]{1,0:T(8,128)(2,1)} %bitcast.30, bf16[256,2560]{1,0:T(8,128)(2,1)} %bitcast.22, bf16[256,256]{1,0:T(8,128)(2,1)} %get-tuple-element.56.bc_ref, f32[40,256]{1,0:T(8,128)} %get-tuple-element.57.log_ref, ...), custom_call_target="tpu_custom_call" | custom-call | flops 8000000000 | bytes 5000000 | tf_op jit(solution)/shard_map/pallas_call | solution.py:442
  35.8 5.0 %all-to-all-done.in_ref = f32[16,8,2688]{2,1,0:T(8,128)S(1)} async-done(((f32[16,8,2688]{2,1,0:T(8,128)}), f32[16,8,2688]{2,1,0:T(8,128)S(1)}, u32[]{:S(2)}, u32[]{:S(2)}) %all-to-all-start) | async-done | bytes 1376288 | tf_op jit(solution)/shard_map/all_to_all | solution.py:439
  40.8 1.1 shard_map.139
  41.9 1.1 copy-done.6
  43.1 7.0 %all-to-all-start.1 = ((f32[16,8,2560]{2,1,0:T(8,128)}), f32[16,8,2560]{2,1,0:T(8,128)}, u32[]{:S(2)}, u32[]{:S(2)}) async-start(f32[16,8,2560]{2,1,0:T(8,128)} %copy-done.6), calls=%async_computation.1 | async-start | bytes 2621440 | tf_op jit(solution)/shard_map/all_to_all | solution.py:468
  50.1 9.5 %shard_map.140 = (f32[256,1280]{1,0:T(8,128)}, f32[256,256]{1,0:T(8,128)}, f32[40,256]{1,0:T(8,128)}, f32[40,256]{1,0:T(8,128)}) custom-call(bf16[256,2560]{1,0:T(8,128)(2,1)} %bitcast.31, bf16[256,2560]{1,0:T(8,128)(2,1)} %bitcast.23, bf16[256,256]{1,0:T(8,128)(2,1)} %get-tuple-element.56.bc_ref, f32[40,256]{1,0:T(8,128)} %get-tuple-element.57.log_ref, ...), custom_call_target="tpu_custom_call" | custom-call | flops 8000000000 | bytes 5000000 | tf_op jit(solution)/shard_map/pallas_call | solution.py:442
  59.6 8.2 %all-to-all-done.1 = f32[16,8,2560]{2,1,0:T(8,128)} async-done(((f32[16,8,2560]{2,1,0:T(8,128)}), f32[16,8,2560]{2,1,0:T(8,128)}, u32[]{:S(2)}, u32[]{:S(2)}) %all-to-all-start.1) | async-done | bytes 1310752 | tf_op jit(solution)/shard_map/all_to_all | solution.py:468
  67.8 1.3 %copy-done.4 = bf16[256,2560]{1,0:T(8,128)(2,1)S(1)} copy-done((bf16[256,2560]{1,0:T(8,128)(2,1)S(1)}, bf16[256,2560]{1,0:T(8,128)(2,1)}, u32[]{:S(2)}) %copy-start.4) | copy-done | bytes 1310744
  69.2 2.5 %shard_map.141 = (bf16[64,2560]{1,0:T(8,128)(2,1)S(1)}, bf16[64,2560]{1,0:T(8,128)(2,1)S(1)}, f32[8,2560]{1,0:T(8,128)S(1)}, f32[256,128]{1,0:T(8,128)S(1)}, f32[8,128]{1,0:T(8,128)S(1)}) custom-call(s32[1]{0:T(128)} %bitcast.core_ref, f32[128,2560]{1,0:T(8,128)} %bitcast.9.chip_ref, f32[128,2688]{1,0:T(8,128)S(1)} %collective-permute-done.got_ref, ...), custom_call_target="tpu_custom_call" | custom-call | flops 400000000 | bytes 6000000 | tf_op jit(solution)/shard_map/pallas_call | solution.py:473
  71.8 1.1 shard_map.142
  73.0 0.6 collective-permute-start.4
  73.7 2.4 %shard_map.144 = (f32[40,256]{1,0:T(8,128)}, f32[8,128]{1,0:T(8,128)S(1)}) custom-call(bf16[128,2560]{1,0:T(8,128)(2,1)S(1)} %get-tuple-element.79.s_ref, bf16[128,2560]{1,0:T(8,128)(2,1)S(1)} %get-tuple-element.89.e_ref, f32[8,2560]{1,0:T(8,128)S(1)} %get-tuple-element.81.meet_ref, bf16[256,2560]{1,0:T(8,128)(2,1)S(1)} %bitcast.32, ...), custom_call_target="tpu_custom_call" | custom-call | flops 400000000 | bytes 4000000 | tf_op jit(solution)/shard_map/pallas_call | solution.py:488
  76.8 0.5 collective-permute-done.5.paramgot_ref
  77.3 1.6 %shard_map.145 = f32[16,88,256]{2,1,0:T(8,128)S(1)} custom-call(f32[1280,256]{1,0:T(8,128)S(1)} %shard_map.143.own_ref, f32[1280,256]{1,0:T(8,128)} %collective-permute-done.2.got_ref, f32[256,256]{1,0:T(8,128)S(1)} %collective-permute-done.4.sggot_ref, f32[8,128]{1,0:T(8,128)S(1)} %get-tuple-element.88.param_ref, ...), custom_call_target="tpu_custom_call" | custom-call | flops 200000000 | bytes 4000000 | tf_op jit(solution)/shard_map/pallas_call | solution.py:500
  79.0 25.4 %all_to_all.15 = f32[16,88,256]{2,1,0:T(8,128)S(1)} all-to-all(f32[16,88,256]{2,1,0:T(8,128)S(1)} %shard_map.145), channel_id=1, replica_groups={{0,16,32,48,64,80,96,112,128,144,160,176,192,208,224,240},{8,24,40,56,7..., dimensions={0} | all-to-all | bytes 2883584 | tf_op jit(solution)/shard_map/all_to_all | solution.py:504
  104.4 2.0 %collective-permute-start.6 = (f32[88,256]{1,0:T(8,128)S(1)}, f32[88,256]{1,0:T(8,128)S(1)}, u32[]{:S(2)}, u32[]{:S(2)}) collective-permute-start(f32[88,256]{1,0:T(8,128)S(1)} %reduce_sum.9), channel_id=1, source_target_pairs={{0,1},{1,0},{2,3},{3,2},{4,5},{5,4},{6,7},{7,6},{8,9},{9,8},{10,11... | collective-permute-start | bytes 270344 | tf_op jit(solution)/shard_map/ppermute | solution.py:539
  106.4 3.0 %shard_map.148 = bf16[256,2560]{1,0:T(8,128)(2,1)} custom-call(bf16[256,256]{1,0:T(8,128)(2,1)} %copy-done.14, bf16[2560,256]{1,0:T(8,128)(2,1)} %proj_ref.1), custom_call_target="tpu_custom_call" | custom-call | flops 1000000000 | bytes 3000000 | tf_op jit(solution)/shard_map/pallas_call | solution.py:534
  109.4 3.4 %collective-permute-start.7 = (f32[88,256]{1,0:T(8,128)S(1)}, f32[88,256]{1,0:T(8,128)S(1)}, u32[]{:S(2)}, u32[]{:S(2)}) collective-permute-start(f32[88,256]{1,0:T(8,128)S(1)} %add.9), channel_id=1, source_target_pairs={{0,2},{1,3},{2,0},{3,1},{4,6},{5,7},{6,4},{7,5},{8,10},{9,11},{10,... | collective-permute-start | bytes 270344 | tf_op jit(solution)/shard_map/ppermute | solution.py:539
  112.8 3.4 %shard_map.146.rest_0_ = bf16[256,2560]{1,0:T(8,128)(2,1)} custom-call(bf16[128,2560]{1,0:T(8,128)(2,1)} %copy-done.1, bf16[256,2560]{1,0:T(8,128)(2,1)} %bitcast.24, bf16[256,256]{1,0:T(8,128)(2,1)} %get-tuple-element.56.bc_ref, f32[40,256]{1,0:T(8,128)} %get-tuple-element.57.log_ref, f32[40,256]{1,0:T(8,128)} %get-tuple-element.63.dt_ref, ...), custom_call_target="tpu_custom_call" | custom-call | flops 1000000000 | bytes 5000000 | tf_op jit(solution)/shard_map/pallas_call | solution.py:516
  116.5 6.5 %collective-permute-start.8 = (f32[88,256]{1,0:T(8,128)S(1)}, f32[88,256]{1,0:T(8,128)S(1)}, u32[]{:S(2)}, u32[]{:S(2)}) collective-permute-start(f32[88,256]{1,0:T(8,128)S(1)} %add.10), channel_id=1, source_target_pairs={{0,4},{1,5},{2,6},{3,7},{4,0},{5,1},{6,2},{7,3},{8,12},{9,13},{10,... | collective-permute-start | bytes 270344 | tf_op jit(solution)/shard_map/ppermute | solution.py:539
  122.9 3.5 %shard_map.147 = bf16[256,2560]{1,0:T(8,128)(2,1)} custom-call(bf16[128,2560]{1,0:T(8,128)(2,1)} %copy-done.1, bf16[256,2560]{1,0:T(8,128)(2,1)} %bitcast.25, bf16[256,256]{1,0:T(8,128)(2,1)} %get-tuple-element.56.bc_ref, f32[40,256]{1,0:T(8,128)} %get-tuple-element.57.log_ref, f32[40,256]{1,0:T(8,128)} %get-tuple-element.63.dt_ref, ...), custom_call_target="tpu_custom_call", output_to_operand_aliasing={{}: (7, {})} | custom-call | flops 1000000000 | bytes 5000000 | tf_op jit(solution)/shard_map/pallas_call | solution.py:516
  126.4 0.5 slice_bitcast_fusion
  126.9 0.6 slice.16
  (56 shorter events, 1.2 us)
Async XLA Ops:
  7.2 3.4 %collective-permute-start = (f32[128,2688]{1,0:T(8,128)}, f32[128,2688]{1,0:T(8,128)S(1)}, u32[]{:S(2)}, u32[]{:S(2)}) collective-permute-start(f32[128,2688]{1,0:T(8,128)} %get-tuple-element.52), channel_id=1, source_target_pairs={{0,8},{8,0},{16,24},{24,16},{32,40},{40,32},{48,56},{56,48},{64,72... | collective-permute-start | bytes 4128776 | tf_op jit(solution)/shard_map/ppermute | solution.py:434
  10.7 1.3 %copy-start.8 = (f32[128,2688]{1,0:T(8,128)S(1)}, f32[128,2688]{1,0:T(8,128)}, u32[]{:S(2)}) copy-start(f32[128,2688]{1,0:T(8,128)} %get-tuple-element.51.keep_ref) | copy-start | bytes 4128772
  13.6 27.2 %all-to-all-start = ((f32[16,8,2688]{2,1,0:T(8,128)}), f32[16,8,2688]{2,1,0:T(8,128)S(1)}, u32[]{:S(2)}, u32[]{:S(2)}) async-start(f32[16,8,2688]{2,1,0:T(8,128)} %bitcast.27), calls=%async_computation | async-start | bytes 2752512 | tf_op jit(solution)/shard_map/all_to_all | solution.py:439
  25.2 24.9 %collective-permute-start.2 = (f32[1280,256]{1,0:T(8,128)}, f32[1280,256]{1,0:T(8,128)}, u32[]{:S(2)}, u32[]{:S(2)}) collective-permute-start(f32[1280,256]{1,0:T(8,128)} %get-tuple-element.62), channel_id=1, source_target_pairs={{0,8},{8,0},{16,24},{24,16},{32,40},{40,32},{48,56},{56,48},{64,72... | collective-permute-start | bytes 3932168 | tf_op jit(solution)/shard_map/ppermute | solution.py:461
  25.2 24.9 %collective-permute-start.1 = (f32[64,2560]{1,0:T(8,128)}, f32[64,2560]{1,0:T(8,128)S(1)}, u32[]{:S(2)}, u32[]{:S(2)}) collective-permute-start(f32[64,2560]{1,0:T(8,128)} %get-tuple-element.61), channel_id=1, source_target_pairs={{0,8},{8,0},{16,24},{24,16},{32,40},{40,32},{48,56},{56,48},{64,72... | collective-permute-start | bytes 1966088 | tf_op jit(solution)/shard_map/ppermute | solution.py:462
  41.9 1.2 copy-start.6
  43.1 24.8 %all-to-all-start.1 = ((f32[16,8,2560]{2,1,0:T(8,128)}), f32[16,8,2560]{2,1,0:T(8,128)}, u32[]{:S(2)}, u32[]{:S(2)}) async-start(f32[16,8,2560]{2,1,0:T(8,128)} %copy-done.6), calls=%async_computation.1 | async-start | bytes 2621440 | tf_op jit(solution)/shard_map/all_to_all | solution.py:468
  50.0 17.8 %copy-start.3 = (bf16[256,2560]{1,0:T(8,128)(2,1)S(1)}, bf16[256,2560]{1,0:T(8,128)(2,1)}, u32[]{:S(2)}) copy-start(bf16[256,2560]{1,0:T(8,128)(2,1)} %get-tuple-element.68.xw_ref) | copy-start | bytes 3932164
  67.8 3.9 %collective-permute-start.3 = (f32[128,2560]{1,0:T(8,128)}, f32[128,2560]{1,0:T(8,128)S(1)}, u32[]{:S(2)}, u32[]{:S(2)}) collective-permute-start(f32[128,2560]{1,0:T(8,128)} %bitcast.9.chip_ref), channel_id=1, source_target_pairs={{0,8},{8,0},{16,24},{24,16},{32,40},{40,32},{48,56},{56,48},{64,72... | collective-permute-start | bytes 3932168 | tf_op jit(solution)/shard_map/ppermute | solution.py:472
  67.8 1.3 %copy-start.4 = (bf16[256,2560]{1,0:T(8,128)(2,1)S(1)}, bf16[256,2560]{1,0:T(8,128)(2,1)}, u32[]{:S(2)}) copy-start(bf16[256,2560]{1,0:T(8,128)(2,1)} %get-tuple-element.69.ge_ref) | copy-start | bytes 3932164
  69.2 2.5 %copy-start.5 = (bf16[256,2560]{1,0:T(8,128)(2,1)S(1)}, bf16[256,2560]{1,0:T(8,128)(2,1)}, u32[]{:S(2)}) copy-start(bf16[256,2560]{1,0:T(8,128)(2,1)} %get-tuple-element.69.ge_ref) | copy-start | bytes 3932164
  69.2 2.5 %copy-start.13 = (f32[256,256]{1,0:T(8,128)S(1)}, f32[256,256]{1,0:T(8,128)}, u32[]{:S(2)}) copy-start(f32[256,256]{1,0:T(8,128)} %get-tuple-element.75.sgin_ref) | copy-start | bytes 786436
  71.7 1.9 %copy-start = (bf16[1,256,2560]{2,1,0:T(8,128)(2,1)S(1)}, bf16[1,256,2560]{2,1,0:T(8,128)(2,1)}, u32[]{:S(2)}) copy-start(bf16[1,256,2560]{2,1,0:T(8,128)(2,1)} %param.11) | copy-start | bytes 3932164
  71.7 1.9 %copy-start.7 = (bf16[1,256,2560]{2,1,0:T(8,128)(2,1)S(1)}, bf16[1,256,2560]{2,1,0:T(8,128)(2,1)}, u32[]{:S(2)}) copy-start(bf16[1,256,2560]{2,1,0:T(8,128)(2,1)} %param.9) | copy-start | bytes 3932164
  71.7 1.9 %copy-start.9 = (bf16[256,256]{1,0:T(8,128)(2,1)S(1)}, bf16[256,256]{1,0:T(8,128)(2,1)}, u32[]{:S(2)}) copy-start(bf16[256,256]{1,0:T(8,128)(2,1)} %get-tuple-element.56.bc_ref) | copy-start | bytes 393220
  71.7 1.9 %copy-start.11 = (f32[40,256]{1,0:T(8,128)S(1)}, f32[40,256]{1,0:T(8,128)}, u32[]{:S(2)}) copy-start(f32[40,256]{1,0:T(8,128)} %get-tuple-element.57.log_ref) | copy-start | bytes 122884
  71.8 1.9 %copy-start.12 = (f32[40,256]{1,0:T(8,128)S(1)}, f32[40,256]{1,0:T(8,128)}, u32[]{:S(2)}) copy-start(f32[40,256]{1,0:T(8,128)} %get-tuple-element.63.dt_ref) | copy-start | bytes 122884
  71.8 1.9 %copy-start.15 = (f32[40,256]{1,0:T(8,128)S(1)}, f32[40,256]{1,0:T(8,128)}, u32[]{:S(2)}) copy-start(f32[40,256]{1,0:T(8,128)} %get-tuple-element.82.sig_ref) | copy-start | bytes 122884
  71.8 1.9 %copy-start.16 = (f32[40,256]{1,0:T(8,128)S(1)}, f32[40,256]{1,0:T(8,128)}, u32[]{:S(2)}) copy-start(f32[40,256]{1,0:T(8,128)} %get-tuple-element.83.crossa_ref) | copy-start | bytes 122884
  71.8 1.9 %copy-start.17 = (f32[40,256]{1,0:T(8,128)S(1)}, f32[40,256]{1,0:T(8,128)}, u32[]{:S(2)}) copy-start(f32[40,256]{1,0:T(8,128)} %get-tuple-element.85.cola_ref) | copy-start | bytes 122884
  71.8 1.9 %copy-start.18 = (f32[40,256]{1,0:T(8,128)S(1)}, f32[40,256]{1,0:T(8,128)}, u32[]{:S(2)}) copy-start(f32[40,256]{1,0:T(8,128)} %get-tuple-element.84.crossb_ref) | copy-start | bytes 122884
  71.8 1.9 %copy-start.19 = (f32[40,256]{1,0:T(8,128)S(1)}, f32[40,256]{1,0:T(8,128)}, u32[]{:S(2)}) copy-start(f32[40,256]{1,0:T(8,128)} %get-tuple-element.86.colb_ref) | copy-start | bytes 122884
  71.8 1.9 %copy-start.20 = (f32[8,128]{1,0:T(8,128)S(1)}, f32[8,128]{1,0:T(8,128)}, u32[]{:S(2)}) copy-start(f32[8,128]{1,0:T(8,128)} %get-tuple-element.87.skip_ref) | copy-start | bytes 12292
  71.8 1.9 %copy-start.21 = (f32[40]{0:T(128)S(1)}, f32[40]{0:T(128)}, u32[]{:S(2)}) copy-start(f32[40]{0:T(128)} %param.14) | copy-start | bytes 484
  73.0 3.2 %copy-start.1 = (bf16[128,2560]{1,0:T(8,128)(2,1)}, bf16[128,2560]{1,0:T(8,128)(2,1)S(1)}, u32[]{:S(2)}) copy-start(bf16[128,2560]{1,0:T(8,128)(2,1)S(1)} %get-tuple-element.89.e_ref) | copy-start | bytes 1966084
  73.0 3.5 %copy-start.14 = (bf16[256,256]{1,0:T(8,128)(2,1)}, bf16[256,256]{1,0:T(8,128)(2,1)S(1)}, u32[]{:S(2)}) copy-start(bf16[256,256]{1,0:T(8,128)(2,1)S(1)} %get-tuple-element.93.sg_ref) | copy-start | bytes 393220
  73.0 4.3 %collective-permute-start.4 = (f32[256,256]{1,0:T(8,128)S(1)}, f32[256,256]{1,0:T(8,128)S(1)}, u32[]{:S(2)}, u32[]{:S(2)}) collective-permute-start(f32[256,256]{1,0:T(8,128)S(1)} %get-tuple-element.78), channel_id=1, source_target_pairs={{0,8},{8,0},{16,24},{24,16},{32,40},{40,32},{48,56},{56,48},{64,72... | collective-permute-start | bytes 786440 | tf_op jit(solution)/shard_map/ppermute | solution.py:487
  73.7 2.8 %copy-start.10 = (bf16[1280,256]{1,0:T(8,128)(2,1)S(1)}, bf16[1280,256]{1,0:T(8,128)(2,1)}, u32[]{:S(2)}) copy-start(bf16[1280,256]{1,0:T(8,128)(2,1)} %get-tuple-element.54.keep_ref) | copy-start | bytes 1966084
  76.2 1.2 collective-permute-start.5
  104.4 5.0 %collective-permute-start.6 = (f32[88,256]{1,0:T(8,128)S(1)}, f32[88,256]{1,0:T(8,128)S(1)}, u32[]{:S(2)}, u32[]{:S(2)}) collective-permute-start(f32[88,256]{1,0:T(8,128)S(1)} %reduce_sum.9), channel_id=1, source_target_pairs={{0,1},{1,0},{2,3},{3,2},{4,5},{5,4},{6,7},{7,6},{8,9},{9,8},{10,11... | collective-permute-start | bytes 270344 | tf_op jit(solution)/shard_map/ppermute | solution.py:539
  109.4 7.0 %collective-permute-start.7 = (f32[88,256]{1,0:T(8,128)S(1)}, f32[88,256]{1,0:T(8,128)S(1)}, u32[]{:S(2)}, u32[]{:S(2)}) collective-permute-start(f32[88,256]{1,0:T(8,128)S(1)} %add.9), channel_id=1, source_target_pairs={{0,2},{1,3},{2,0},{3,1},{4,6},{5,7},{6,4},{7,5},{8,10},{9,11},{10,... | collective-permute-start | bytes 270344 | tf_op jit(solution)/shard_map/ppermute | solution.py:539
  116.5 9.9 %collective-permute-start.8 = (f32[88,256]{1,0:T(8,128)S(1)}, f32[88,256]{1,0:T(8,128)S(1)}, u32[]{:S(2)}, u32[]{:S(2)}) collective-permute-start(f32[88,256]{1,0:T(8,128)S(1)} %add.10), channel_id=1, source_target_pairs={{0,4},{1,5},{2,6},{3,7},{4,0},{5,1},{6,2},{7,3},{8,12},{9,13},{10,... | collective-permute-start | bytes 270344 | tf_op jit(solution)/shard_map/ppermute | solution.py:539
  (1 other events, 1.1 us)
